TPU v7x, 32 devices: a whole 2x2x4 slice. The times are simulated.
32 devices in a mesh: hop: 16 (over z, y, x), par: 2 (over core).
Axes of the slice: x: 2, y: 2, z: 4, core: 2. Of those that a mesh axis runs over, the one named last changes fastest.
Arguments:
- child_feats: bfloat16 [16384, 1024], P(('hop', 'par')), may hold values from -6 to 6
- board_mask: int32 [16384], P(('hop', 'par')), may hold values 0 or 1
- importance: float32 [16384], P(('hop', 'par')), may hold values from 0.1 to 1
- parent_slot: int32 [16384], P(('hop', 'par')), may hold values from 0 to 1023
- send_counts: int32 [32, 32], P(('hop', 'par')), may hold values from 1 to 16, as said below
- parent_feats: bfloat16 [32768, 1024], P(('hop', 'par')), may hold values from -6 to 6
- proj_weight: bfloat16 [1024, 1024], replicated, may hold values from -0.1875 to 0.1875
- q_weight: bfloat16 [1024, 1024], replicated, may hold values from -0.1875 to 0.1875
- q_bias: float32 [1024], replicated, may hold values from -1.5 to 1.5
- w_weight: bfloat16 [2048, 1024], replicated, may hold values from -0.125 to 0.125
- w_bias: float32 [1024], replicated, may hold values from -1.5 to 1.5
- emb_cotangent: float32 [32768, 1024], P(('hop', 'par')), may hold values from -6 to 6
Outputs:
- embedding: float32 [32768, 1024], P(('hop', 'par'))
- grad_child: bfloat16 [16384, 1024], P(('hop', 'par'))
- grad_parent: float32 [32768, 1024], P(('hop', 'par'))
- grad_proj: float32 [1024, 1024], replicated
- grad_q: float32 [1024, 1024], replicated
- grad_qbias: float32 [1024], replicated
- grad_w: float32 [2048, 1024], replicated
- grad_wbias: float32 [1024], replicated
Inputs may be any that keep to these rules, and one draw needn't show every extreme that they name: `send_counts`: in every draw one parent owner receives 16 live slots from every source device.
All inputs are finite; a program needn't handle non-finite values. No bound on the sum of `board_mask` on one device may be relied on, other than what follows from the above.
Results may differ from a plain program's by a relative error of at most 0.0068.
Values may be sent and summed in bfloat16 or wider, within the bound.
A program may use at most 192 MiB of HBM per device.

v0:
```python
import jax
import jax.numpy as jnp
from jax import lax
from jax.sharding import PartitionSpec as P


def times_transpose(left, right):
    return lax.dot_general(
        left, right, (((1,), (1,)), ((), ())), preferred_element_type=jnp.float32
    )


def contract_rows(left, right):
    return lax.dot_general(
        left, right, (((0,), (0,)), ((), ())), preferred_element_type=jnp.float32
    )


def silu_slope(value):
    sigma = jax.nn.sigmoid(value)
    return sigma * (1.0 + value * (1.0 - sigma))


def send_rows(payload, hop_count, par_count, slot_cap, feature_width):
    parcel = payload.reshape(hop_count * par_count, slot_cap, feature_width)
    arrived = lax.all_to_all(parcel, ("hop", "par"), split_axis=0, concat_axis=0, tiled=True)
    return arrived.reshape(payload.shape)


def send_back(payload, hop_count, par_count, slot_cap, feature_width):
    parcel = payload.reshape(hop_count * par_count, slot_cap, feature_width)
    arrived = lax.all_to_all(parcel, ("hop", "par"), split_axis=0, concat_axis=0, tiled=True)
    return arrived.reshape(payload.shape)


def body(
    child_feats,
    board_mask,
    importance,
    parent_slot,
    send_counts,
    parent_feats,
    proj_weight,
    q_weight,
    q_bias,
    w_weight,
    w_bias,
    emb_cotangent,
):
    slot_rows, feature_width = child_feats.shape
    hop_count = lax.axis_size("hop")
    par_count = lax.axis_size("par")
    shard_count = hop_count * par_count
    slot_cap = slot_rows // shard_count
    live_slots = (
        (jnp.arange(slot_cap)[None, :] < send_counts[0][:, None])
        .astype(jnp.float32)
        .reshape(slot_rows)
    )
    weight_live = importance * live_slots
    is_board = board_mask[:, None] == 1
    projected = jnp.dot(child_feats, proj_weight, preferred_element_type=jnp.float32)
    merged = jnp.where(is_board, projected, child_feats.astype(jnp.float32)).astype(jnp.bfloat16)
    pre_act = jnp.dot(merged, q_weight, preferred_element_type=jnp.float32) + q_bias
    message = (weight_live[:, None] * jax.nn.silu(pre_act)).astype(jnp.bfloat16)
    edge_info = jnp.stack([weight_live, parent_slot.astype(jnp.float32)]).reshape(
        2, shard_count, slot_cap
    )
    got_info = lax.all_to_all(edge_info, ("hop", "par"), split_axis=1, concat_axis=1, tiled=True)
    got_weight = got_info[0].reshape(slot_rows)
    got_slot = got_info[1].reshape(slot_rows).astype(jnp.int32)
    arrived = send_rows(message, hop_count, par_count, slot_cap, feature_width)
    parent_rows = parent_feats.shape[0]
    owner_table = got_slot[None, :] == jnp.arange(parent_rows, dtype=jnp.int32)[:, None]
    gathered = jnp.dot(
        owner_table.astype(jnp.bfloat16), arrived, preferred_element_type=jnp.float32
    )
    weight_sum = jnp.sum(jnp.where(owner_table, got_weight[None, :], 0.0), axis=1)
    divisor = jnp.maximum(weight_sum, 1.0)
    neighbor_mean = (gathered / divisor[:, None]).astype(jnp.bfloat16)
    joined = jnp.concatenate([parent_feats, neighbor_mean], axis=1)
    pre_norm = jnp.dot(joined, w_weight, preferred_element_type=jnp.float32) + w_bias
    act_out = jax.nn.silu(pre_norm)
    inv_norm = lax.rsqrt(jnp.sum(act_out * act_out, axis=1, keepdims=True) + 1e-06)
    embedding = act_out * inv_norm
    grad_emb = inv_norm * (
        emb_cotangent - embedding * jnp.sum(emb_cotangent * embedding, axis=1, keepdims=True)
    )
    grad_pre = (grad_emb * silu_slope(pre_norm)).astype(jnp.bfloat16)
    grad_w = contract_rows(joined, grad_pre)
    grad_wbias = jnp.sum(grad_pre.astype(jnp.float32), axis=0)
    grad_cat = times_transpose(grad_pre, w_weight)
    grad_parent = grad_cat[:, :feature_width]
    grad_mean = grad_cat[:, feature_width:] / divisor[:, None]
    return_rows = jnp.take(grad_mean, got_slot, axis=0).astype(jnp.bfloat16)
    grad_message = send_back(return_rows, hop_count, par_count, slot_cap, feature_width)
    again_pre = jnp.dot(merged, q_weight, preferred_element_type=jnp.float32) + q_bias
    grad_act = weight_live[:, None] * grad_message.astype(jnp.float32)
    grad_preact = (grad_act * silu_slope(again_pre)).astype(jnp.bfloat16)
    grad_q = contract_rows(merged, grad_preact)
    grad_qbias = jnp.sum(grad_preact.astype(jnp.float32), axis=0)
    grad_merged = times_transpose(grad_preact, q_weight)
    grad_board = jnp.where(is_board, grad_merged, 0.0).astype(jnp.bfloat16)
    grad_proj = contract_rows(child_feats, grad_board)
    grad_child = (
        jnp.where(is_board, 0.0, grad_merged) + times_transpose(grad_board, proj_weight)
    ).astype(jnp.bfloat16)
    summed = lax.psum((grad_proj, grad_q, grad_qbias, grad_w, grad_wbias), ("hop", "par"))
    return (
        embedding,
        grad_child,
        grad_parent,
        summed[0],
        summed[1],
        summed[2],
        summed[3],
        summed[4],
    )


def solution(mesh):
    placed = (
        P(("hop", "par"), None),
        P(("hop", "par")),
        P(("hop", "par")),
        P(("hop", "par")),
        P(("hop", "par"), None),
        P(("hop", "par"), None),
        P(),
        P(),
        P(),
        P(),
        P(),
        P(("hop", "par"), None),
    )
    return jax.shard_map(
        body,
        mesh=mesh,
        in_specs=placed,
        out_specs=(
            P(("hop", "par"), None),
            P(("hop", "par"), None),
            P(("hop", "par"), None),
            P(),
            P(),
            P(),
            P(),
            P(),
        ),
        check_vma=False,
    )
```

profile of v0, /device:TPU:0, one launch (start us, length us, event | category | flops | bytes accessed | tf_op | source)
XLA Modules:
  0.0 444.0 jit_solution(8879017638084517741)
XLA Ops:
  10.3 7.3 %all-to-all-start = ((f32[2,32,16]{2,0,1:T(2,128)}), f32[2,32,16]{2,0,1:T(2,128)S(1)}, u32[]{:S(2)}, u32[]{:S(2)}) async-start(f32[2,32,16]{2,0,1:T(2,128)} %copy.42), calls=%async_computation | async-start | bytes 65536 | tf_op jit(solution)/shard_map/all_to_all | solution.py:69
  18.3 3.4 select_convert_fusion.2
  22.8 3.1 multiply_convert_fusion.1
  26.0 6.0 %all-to-all-start.1 = ((bf16[32,16,1024]{2,1,0:T(8,128)(2,1)}), bf16[32,16,1024]{2,1,0:T(8,128)(2,1)S(1)}, u32[]{:S(2)}, u32[]{:S(2)}) async-start(bf16[32,16,1024]{2,1,0:T(8,128)(2,1)} %bitcast.1), calls=%async_computation.1 | async-start | bytes 2097152 | tf_op jit(solution)/shard_map/all_to_all | solution.py:26
  32.0 3.9 copy.43
  35.9 5.3 %copy.45 = f32[1024,1024]{0,1:T(8,128)} copy(f32[1024,1024]{1,0:T(8,128)} %param.23) | data formatting | bytes 8388608 | tf_op args[11]
  42.0 16.1 %all-to-all-done.1 = bf16[32,16,1024]{2,1,0:T(8,128)(2,1)S(1)} async-done(((bf16[32,16,1024]{2,1,0:T(8,128)(2,1)}), bf16[32,16,1024]{2,1,0:T(8,128)(2,1)S(1)}, u32[]{:S(2)}, u32[]{:S(2)}) %all-to-all-start.1) | async-done | bytes 1048608 | tf_op jit(solution)/shard_map/all_to_all | solution.py:26
  58.0 1.3 divide_convert_fusion
  60.9 5.6 %multiply_reduce_fusion.1 = (f32[1024]{0:T(1024)S(1)}, f32[1024,1024]{0,1:T(8,128)S(1)}) fusion(f32[1024]{0:T(1024)S(1)} %copy-done.9, bf16[2048,1024]{1,0:T(8,128)(2,1)S(1)} %copy-done.11, bf16[1024,1024]{0,1:T(8,128)(2,1)S(1)} %divide_convert_fusion, bf16[1024,1024]{0,1:T(8,128)(2,1)S(1)} %copy-done.4), kind=kOutput, calls=%fused_computation.5 | convolution fusion | flops 4310694912 | bytes 12591104 | tf_op jit(solution)/shard_map/dot_general | solution.py:82
  66.5 1.8 multiply_reduce_fusion
  68.4 4.4 convert_reduce_fusion
  72.8 1.3 copy-done.5
  74.1 4.6 %fusion.16 = f32[1024,2048]{1,0:T(8,128)S(1)} fusion(bf16[1024,1024]{0,1:T(8,128)(2,1)S(1)} %get-tuple-element.46, bf16[2048,1024]{1,0:T(8,128)(2,1)S(1)} %copy-done.11), kind=kOutput, calls=%fused_computation.48 | convolution fusion | flops 4294967296 | bytes 14680064 | tf_op jit(solution)/shard_map/dot_general | solution.py:8
  78.7 4.2 fusion.15
  83.0 5.3 %copy.50 = f32[1024,1024]{0,1:T(8,128)} copy(f32[1024,1024]{1,0:T(8,128)} %get-tuple-element.50) | data formatting | bytes 8388608
  88.3 4.1 broadcast_divide_fusion
  92.4 3.9 copy.47
  96.3 4.6 %gather_fusion = bf16[512,1024]{1,0:T(8,128)(2,1)S(1)} fusion(bf16[1024,1024]{1,0:T(8,128)(2,1)} %copy.47, s32[1024]{0:T(1024)S(1)} %pad_clamp_fusion), kind=kCustom, calls=%fused_computation | custom fusion | bytes 2099200 | tf_op jit(solution)/shard_map/jit(_take)/gather | solution.py:95
  102.2 3.6 all-to-all-start.2
  106.1 10.8 %fusion.1 = f32[2048,1024]{1,0:T(8,128)} fusion(bf16[1024,1024]{0,1:T(8,128)(2,1)} %copy-done.5, bf16[1024,1024]{0,1:T(8,128)(2,1)} %copy-done.12, bf16[1024,1024]{0,1:T(8,128)(2,1)} %copy.43), kind=kOutput, calls=%fused_computation.9 | convolution fusion | flops 4303355904 | bytes 14680064 | tf_op jit(solution)/shard_map/dot_general | solution.py:14
  116.9 15.1 %all-to-all-done.2 = bf16[32,16,1024]{2,1,0:T(8,128)(2,1)S(1)} async-done(((bf16[32,16,1024]{2,1,0:T(8,128)(2,1)}), bf16[32,16,1024]{2,1,0:T(8,128)(2,1)S(1)}, u32[]{:S(2)}, u32[]{:S(2)}) %all-to-all-start.2) | async-done | bytes 1048608 | tf_op jit(solution)/shard_map/all_to_all | solution.py:32
  132.0 2.6 convert_reduce_fusion.1
  134.6 1.3 fusion.17
  135.9 3.2 fusion.18
  139.2 3.4 convolution_bitcast_fusion
  142.6 5.3 %copy.48 = f32[1024,1024]{1,0:T(8,128)} copy(f32[1024,1024]{0,1:T(8,128)} %get-tuple-element.51) | data formatting | bytes 8388608
  148.0 40.3 %all-reduce = (f32[1024]{0:T(1024)}, f32[1024]{0:T(1024)}) all-reduce(f32[1024]{0:T(1024)S(1)} %get-tuple-element.47, f32[1024]{0:T(1024)S(1)} %get-tuple-element.45), channel_id=1, replica_groups=mesh['hop'=16,'par'=2] {'hop','par'}, use_global_device_ids=true, to_apply=%region_6.7 | all-reduce | flops 2048 | bytes 16384 | tf_op jit(solution)/shard_map/psum | solution.py:108
  188.2 5.8 %add_convert_fusion = bf16[512,1024]{1,0:T(8,128)(2,1)} fusion(f32[512,1024]{1,0:T(8,128)} %copy-done.3, bf16[1024,1024]{1,0:T(8,128)(2,1)} %param.18, pred[512]{0:T(512)(128)(4,1)S(1)} %broadcast_compare_fusion), kind=kOutput, calls=%fused_computation.16 | convolution fusion | flops 1076363264 | bytes 5243392 | tf_op jit(solution)/shard_map/dot_general | solution.py:8
  194.0 228.3 %all-reduce.4.cloned.1.call-done = (f32[1024,1024]{0,1:T(8,128)}, f32[1024,1024]{1,0:T(8,128)}, f32[2048,1024]{1,0:T(8,128)}) async-done(((f32[1024,1024]{0,1:T(8,128)}, f32[1024,1024]{1,0:T(8,128)}, f32[2048,1024]{1,0:T(8,128)}), (f32[1024,1024]{0,1:T(8,128)}, f32[1024,1024]{1,0:T(8,128)}, f32[2048,1024]{1,0:T(8,128)})) %all-reduce.4.cloned.1.call-update) | async-done | bytes 16777232 | tf_op jit(solution)/shard_map/psum | solution.py:108
  422.3 5.3 %copy.49 = f32[1024,1024]{1,0:T(8,128)} copy(f32[1024,1024]{0,1:T(8,128)} %get-tuple-element.42) | data formatting | bytes 8388608
  427.6 5.1 %copy.54 = f32[1024,1024]{1,0:T(8,128)} copy(f32[1024,1024]{1,0:T(8,128)} %get-tuple-element.62) | data formatting | bytes 8388608
  433.7 3.4 copy.55
  (49 shorter events, 9.7 us)
Async XLA Ops:
  7.2 15.7 %copy-start = (bf16[1024,1024]{1,0:T(8,128)(2,1)S(1)}, bf16[1024,1024]{1,0:T(8,128)(2,1)}, u32[]{:S(2)}) copy-start(bf16[1024,1024]{1,0:T(8,128)(2,1)} %param.19) | copy-start | bytes 6291460
  10.3 15.6 %all-to-all-start = ((f32[2,32,16]{2,0,1:T(2,128)}), f32[2,32,16]{2,0,1:T(2,128)S(1)}, u32[]{:S(2)}, u32[]{:S(2)}) async-start(f32[2,32,16]{2,0,1:T(2,128)} %copy.42), calls=%async_computation | async-start | bytes 65536 | tf_op jit(solution)/shard_map/all_to_all | solution.py:69
  18.3 4.5 %copy-start.10 = (f32[1024]{0:T(1024)S(1)}, f32[1024]{0:T(1024)}, u32[]{:S(2)}) copy-start(f32[1024]{0:T(1024)} %param.20) | copy-start | bytes 12292
  21.8 1.0 copy-start.6
  26.0 32.1 %all-to-all-start.1 = ((bf16[32,16,1024]{2,1,0:T(8,128)(2,1)}), bf16[32,16,1024]{2,1,0:T(8,128)(2,1)S(1)}, u32[]{:S(2)}, u32[]{:S(2)}) async-start(bf16[32,16,1024]{2,1,0:T(8,128)(2,1)} %bitcast.1), calls=%async_computation.1 | async-start | bytes 2097152 | tf_op jit(solution)/shard_map/all_to_all | solution.py:26
  58.0 1.6 copy-start.4
  58.0 1.6 copy-start.9
  58.0 2.8 copy-start.11
  60.9 5.6 %copy-start.12 = (bf16[1024,1024]{0,1:T(8,128)(2,1)}, bf16[1024,1024]{0,1:T(8,128)(2,1)S(1)}, u32[]{:S(2)}) copy-start(bf16[1024,1024]{0,1:T(8,128)(2,1)S(1)} %divide_convert_fusion) | copy-start | bytes 6291460
  60.9 5.6 %copy-start.1 = (f32[1024,1024]{0,1:T(8,128)S(1)}, f32[1024,1024]{0,1:T(8,128)}, u32[]{:S(2)}) copy-start(f32[1024,1024]{0,1:T(8,128)} %copy.45) | copy-start | bytes 12582916
  72.8 1.3 copy-start.5
  102.2 29.9 %all-to-all-start.2 = ((bf16[32,16,1024]{2,1,0:T(8,128)(2,1)}), bf16[32,16,1024]{2,1,0:T(8,128)(2,1)S(1)}, u32[]{:S(2)}, u32[]{:S(2)}) async-start(bf16[32,16,1024]{2,1,0:T(8,128)(2,1)} %select_convert_fusion.1), calls=%async_computation.2 | async-start | bytes 2097152 | tf_op jit(solution)/shard_map/all_to_all | solution.py:32
  105.8 316.5 %all-reduce.4.cloned.1.call-start = ((), (), s32[]{:S(2)}) async-start(), calls=%async_computation.3 | async-start | bytes 33554432 | tf_op jit(solution)/shard_map/psum | solution.py:108
  134.6 1.3 copy-start.7
  135.9 3.3 copy-start.3
  135.9 3.2 copy-start.8
  427.6 6.2 %copy-start.2 = (f32[2048,1024]{1,0:T(8,128)S(1)}, f32[2048,1024]{1,0:T(8,128)}, u32[]{:S(2)}) copy-start(f32[2048,1024]{1,0:T(8,128)} %get-tuple-element.64) | copy-start | bytes 25165828
Sparse Core Ops, SparseCore 0:
  142.7 279.4 all-reduce.3
where the time goes:
time: 445 us; the launch traced here: 444 us
  waiting for transfers between devices  259 us (58%)
  local copies, waits for them, and re-layouts  52.6 us (12%)
  matrix products  42.6 us (10%)
  blocking collectives  40.3 us (9%)
  other arithmetic  17.6 us (4%)
  starting transfers between devices  17.2 us (4%)
  between operations  14.2 us (3%)
    psum x1, waiting for transfers between devices, body(): lax.psum((grad_proj, grad_q, grad_qbias, grad_w, grad_wbias), ('hop', 'pa...  228 us
    psum x1, blocking collectives, body(): lax.psum((grad_proj, grad_q, grad_qbias, grad_w, grad_wbias), ('hop', 'pa...  40.3 us
    unnamed x33, local copies, waits for them, and re-layouts  38.8 us
    dot_general x3, matrix products, contract_rows(): lax.dot_general(left, right, (((0,), (0,)), ((), ())), preferred_element_...  17.5 us
    all_to_all x1, waiting for transfers between devices, send_rows(): lax.all_to_all(parcel, ('hop', 'par'), split_axis=0, concat_axis=0, tiled...  16.1 us
    all_to_all x1, waiting for transfers between devices, send_back(): lax.all_to_all(parcel, ('hop', 'par'), split_axis=0, concat_axis=0, tiled...  15.1 us
    dot_general x3, matrix products, times_transpose(): lax.dot_general(left, right, (((1,), (1,)), ((), ())), preferred_element_...  11.6 us
  transfers between devices with their start and end apart: 4, of which 3 were waited for; matrix products, arithmetic and copies ran while one was open for 9% of the time, Pallas kernels for 0%

commit v1 on v0

--- a/solution.py
+++ b/solution.py
@@ -1,7 +1,14 @@
+import functools
+
 import jax
 import jax.numpy as jnp
 from jax import lax
+from jax.experimental import pallas as pl
+from jax.experimental.pallas import tpu as pltpu
 from jax.sharding import PartitionSpec as P
+
+MESH = pl.DeviceIdType.MESH
+CORE = -1
 
 
 def times_transpose(left, right):
@@ -27,10 +34,125 @@
     return arrived.reshape(payload.shape)
 
 
-def send_back(payload, hop_count, par_count, slot_cap, feature_width):
-    parcel = payload.reshape(hop_count * par_count, slot_cap, feature_width)
-    arrived = lax.all_to_all(parcel, ("hop", "par"), split_axis=0, concat_axis=0, tiled=True)
-    return arrived.reshape(payload.shape)
+def halving_orders(hop_count, rows):
+    bits = hop_count.bit_length() - 1
+    if bits == 4:
+        x, y, z0, z1 = range(4)
+        base = [[x, y, z0, z1], [y, x, z0, z1], [z0, x, y, z1], [x, y, z0, z1]]
+        base += [[y, x, z0, z1], [z0, y, x, z1], [x, y, z0, z1], [y, x, z0, z1]]
+    else:
+        base = [[(first + k) % bits for k in range(bits)] for first in range(0, bits, 2)]
+    groups = 1
+    while groups * 2 <= len(base) and rows // (groups * 2) // (hop_count * 2) >= 16:
+        groups *= 2
+    return [[CORE] + order for order in base[:groups]]
+
+
+def own_bit(hop, core, bit):
+    return core if bit == CORE else lax.rem(hop // (1 << bit), 2)
+
+
+def partner(hop, core, bit):
+    if bit == CORE:
+        return (hop, 1 - core)
+    return (hop + (1 - 2 * own_bit(hop, core, bit)) * (1 << bit), core)
+
+
+def sum_kernel(orders, part_ref, sum_ref, held, inbox, send_sem, recv_sem, out_sem, in_sem):
+    hop, core = lax.axis_index("hop"), lax.axis_index("par")
+    groups, levels = len(orders), len(orders[0])
+    rows = part_ref.shape[0] // groups
+    barrier = pltpu.get_barrier_semaphore()
+    for bit in range(CORE, levels - 1):
+        pl.semaphore_signal(barrier, inc=1, device_id=partner(hop, core, bit), device_id_type=MESH)
+    held[...] = part_ref[...]
+    pl.semaphore_wait(barrier, levels)
+
+    start = [jnp.int32(group * rows) for group in range(groups)]
+    kept = [[None] * levels for _ in range(groups)]
+    places = [rows - (rows >> level) for level in range(levels)]
+    down, up = {}, {}
+
+    def halve(group, level):
+        bit = orders[group][level]
+        half = rows >> (level + 1)
+        mine = own_bit(hop, core, bit)
+        away = pl.multiple_of(start[group] + (1 - mine) * half, half)
+        copy = pltpu.make_async_remote_copy(
+            src_ref=held.at[pl.ds(away, half)],
+            dst_ref=inbox.at[group, pl.ds(places[level], half)],
+            send_sem=send_sem.at[group, level],
+            recv_sem=recv_sem.at[group, level],
+            device_id=partner(hop, core, bit),
+            device_id_type=MESH,
+        )
+        copy.start()
+        down[group, level] = copy
+        start[group] = start[group] + mine * half
+        kept[group][level] = start[group]
+
+    def double(group, level):
+        half = rows >> (level + 1)
+        part = pl.ds(pl.multiple_of(kept[group][level], half), half)
+        copy = pltpu.make_async_remote_copy(
+            src_ref=sum_ref.at[part],
+            dst_ref=sum_ref.at[part],
+            send_sem=out_sem.at[group, level],
+            recv_sem=in_sem.at[group, level],
+            device_id=partner(hop, core, orders[group][level]),
+            device_id_type=MESH,
+        )
+        copy.start()
+        up[group, level] = copy
+
+    for group in range(groups):
+        halve(group, 0)
+    for level in range(levels):
+        for group in range(groups):
+            half = rows >> (level + 1)
+            part = pl.ds(pl.multiple_of(kept[group][level], half), half)
+            down[group, level].wait_recv()
+            total = held[part] + inbox[group, pl.ds(places[level], half)]
+            if level < levels - 1:
+                held[part] = total
+                halve(group, level + 1)
+            else:
+                sum_ref[part] = total
+                double(group, level)
+    for level in range(levels - 1, -1, -1):
+        for group in range(groups):
+            up[group, level].wait_recv()
+            if level > 0:
+                double(group, level - 1)
+    for level in range(levels):
+        for group in range(groups):
+            down[group, level].wait_send()
+            up[group, level].wait_send()
+
+
+def sum_over_devices(part, hop_count):
+    rows, columns = part.shape
+    orders = halving_orders(hop_count, rows)
+    groups, levels = len(orders), len(orders[0])
+    semaphores = pltpu.SemaphoreType.DMA((groups, levels))
+    return pl.pallas_call(
+        functools.partial(sum_kernel, orders),
+        name="weight_gradient_sum",
+        out_shape=jax.ShapeDtypeStruct((rows, columns), part.dtype),
+        in_specs=[pl.BlockSpec(memory_space=pltpu.VMEM)],
+        out_specs=pl.BlockSpec(memory_space=pltpu.VMEM),
+        scratch_shapes=[
+            pltpu.VMEM((rows, columns), part.dtype),
+            pltpu.VMEM((groups, rows // groups, columns), part.dtype),
+            semaphores,
+            semaphores,
+            semaphores,
+            semaphores,
+        ],
+        compiler_params=pltpu.CompilerParams(
+            collective_id=0, has_side_effects=True, vmem_limit_bytes=48 << 20
+        ),
+    )(part)
 
 
 def body(
@@ -93,10 +215,9 @@
     grad_parent = grad_cat[:, :feature_width]
     grad_mean = grad_cat[:, feature_width:] / divisor[:, None]
     return_rows = jnp.take(grad_mean, got_slot, axis=0).astype(jnp.bfloat16)
-    grad_message = send_back(return_rows, hop_count, par_count, slot_cap, feature_width)
-    again_pre = jnp.dot(merged, q_weight, preferred_element_type=jnp.float32) + q_bias
+    grad_message = send_rows(return_rows, hop_count, par_count, slot_cap, feature_width)
     grad_act = weight_live[:, None] * grad_message.astype(jnp.float32)
-    grad_preact = (grad_act * silu_slope(again_pre)).astype(jnp.bfloat16)
+    grad_preact = (grad_act * silu_slope(pre_act)).astype(jnp.bfloat16)
     grad_q = contract_rows(merged, grad_preact)
     grad_qbias = jnp.sum(grad_preact.astype(jnp.float32), axis=0)
     grad_merged = times_transpose(grad_preact, q_weight)
@@ -105,47 +226,30 @@
     grad_child = (
         jnp.where(is_board, 0.0, grad_merged) + times_transpose(grad_board, proj_weight)
     ).astype(jnp.bfloat16)
-    summed = lax.psum((grad_proj, grad_q, grad_qbias, grad_w, grad_wbias), ("hop", "par"))
+    part = jnp.concatenate([grad_w, grad_q, grad_proj]).astype(jnp.bfloat16)
+    summed = sum_over_devices(part, hop_count)
+    summed = summed.astype(jnp.float32)
+    grad_qbias, grad_wbias = lax.psum((grad_qbias, grad_wbias), ("hop", "par"))
+    w_rows, q_rows = grad_w.shape[0], grad_q.shape[0]
     return (
         embedding,
         grad_child,
         grad_parent,
-        summed[0],
-        summed[1],
-        summed[2],
-        summed[3],
-        summed[4],
+        summed[w_rows + q_rows :],
+        summed[w_rows : w_rows + q_rows],
+        grad_qbias,
+        summed[:w_rows],
+        grad_wbias,
     )
 
 
 def solution(mesh):
-    placed = (
-        P(("hop", "par"), None),
-        P(("hop", "par")),
-        P(("hop", "par")),
-        P(("hop", "par")),
-        P(("hop", "par"), None),
-        P(("hop", "par"), None),
-        P(),
-        P(),
-        P(),
-        P(),
-        P(),
-        P(("hop", "par"), None),
-    )
+    rows = P(("hop", "par"), None)
+    flat = P(("hop", "par"))
     return jax.shard_map(
         body,
         mesh=mesh,
-        in_specs=placed,
-        out_specs=(
-            P(("hop", "par"), None),
-            P(("hop", "par"), None),
-            P(("hop", "par"), None),
-            P(),
-            P(),
-            P(),
-            P(),
-            P(),
-        ),
+        in_specs=(rows, flat, flat, flat, rows, rows, P(), P(), P(), P(), P(), rows),
+        out_specs=(rows, rows, rows, P(), P(), P(), P(), P()),
         check_vma=False,
     )

time: 445 us -> 293 us (0.66)
  waiting for transfers between devices: 259 us -> 27.7 us
  Pallas kernels: 0 us -> 100 us
  between operations: 14.2 us -> 1.14 us
  matrix products: 42.6 us -> 33.8 us
    psum x1 -> x0, waiting for transfers between devices: 228 us -> none  [body(): lax.psum((grad_proj, grad_q, grad_qbias, grad_w, grad_wbias), ('hop', 'pa...]
    pallas_call x0 -> x1, Pallas kernels: none -> 100 us  [sum_over_devices(): pl.pallas_call(functools.partial(sum_kernel, orders), name='weight_gradie...]
    all_to_all x1 -> x0, waiting for transfers between devices: 15.1 us -> none  [send_back(): lax.all_to_all(parcel, ('hop', 'par'), split_axis=0, concat_axis=0, tiled...]
    unnamed x33 -> x32, local copies, waits for them, and re-layouts: 38.8 us -> 24.9 us
    all_to_all x1 -> x2, waiting for transfers between devices: 16.1 us -> 27.7 us  [send_rows(): lax.all_to_all(parcel, ('hop', 'par'), split_axis=0, concat_axis=0, tiled...]
    slice x0 -> x2, local copies, waits for them, and re-layouts: none -> 11.2 us  [the longest x1 6.8 us: body(): summed[:w_rows]]
    dot_general x3, matrix products: 17.5 us -> 12.1 us  [contract_rows(): lax.dot_general(left, right, (((0,), (0,)), ((), ())), preferred_element_...]
    all_to_all x1 -> x2, starting transfers between devices: 6.01 us -> 10.2 us  [send_rows(): lax.all_to_all(parcel, ('hop', 'par'), split_axis=0, concat_axis=0, tiled...]
  transfers between devices with their start and end apart: 4 -> 3, of which waited for: 3 -> 2; matrix products, arithmetic and copies ran while one was open for 9% -> 11% of each run, Pallas kernels for 0% -> 0%
where the time goes in v1:
time: 293 us; the launch traced here: 290 us
  Pallas kernels  100 us (34%)
  local copies, waits for them, and re-layouts  50 us (17%)
  blocking collectives  37.7 us (13%)
  matrix products  33.8 us (12%)
  waiting for transfers between devices  27.7 us (9%)
  other arithmetic  21.9 us (7%)
  starting transfers between devices  17.5 us (6%)
    pallas_call x1, Pallas kernels, sum_over_devices(): pl.pallas_call(functools.partial(sum_kernel, orders), name='weight_gradie...  100 us
    psum x1, blocking collectives, body(): grad_qbias, grad_wbias = lax.psum((grad_qbias, grad_wbias), ('hop', 'par'))  37.7 us
    all_to_all x2, waiting for transfers between devices, send_rows(): lax.all_to_all(parcel, ('hop', 'par'), split_axis=0, concat_axis=0, tiled...  27.7 us
    unnamed x32, local copies, waits for them, and re-layouts  24.9 us
    dot_general x3, matrix products, contract_rows(): lax.dot_general(left, right, (((0,), (0,)), ((), ())), preferred_element_...  12.1 us
    all_to_all x2, starting transfers between devices, send_rows(): lax.all_to_all(parcel, ('hop', 'par'), split_axis=0, concat_axis=0, tiled...  10.2 us
    dot_general x3, matrix products, times_transpose(): lax.dot_general(left, right, (((1,), (1,)), ((), ())), preferred_element_...  8.19 us
    all_to_all x1, starting transfers between devices, body(): lax.all_to_all(edge_info, ('hop', 'par'), split_axis=1, concat_axis=1, ti...  7.3 us
  transfers between devices with their start and end apart: 3, of which 2 were waited for; matrix products, arithmetic and copies ran while one was open for 11% of the time, Pallas kernels for 0%

profile of v1, /device:TPU:0, one launch (start us, length us, event | category | flops | bytes accessed | tf_op | source)
XLA Modules:
  0.0 289.7 jit_solution(5295485560963717234)
XLA Ops:
  3.8 7.3 %all-to-all-start = ((f32[2,32,16]{2,0,1:T(2,128)}), f32[2,32,16]{2,0,1:T(2,128)S(1)}, u32[]{:S(2)}, u32[]{:S(2)}) async-start(f32[2,32,16]{2,0,1:T(2,128)} %copy.39), calls=%async_computation | async-start | bytes 65536 | tf_op jit(solution)/shard_map/all_to_all | solution.py:191
  11.8 3.4 %select_convert_fusion.2 = bf16[512,1024]{1,0:T(8,128)(2,1)S(1)} fusion(bf16[512,1024]{1,0:T(8,128)(2,1)} %param.12, bf16[1024,1024]{1,0:T(8,128)(2,1)} %param.18, pred[512]{0:T(512)(128)(4,1)S(1)} %broadcast_compare_fusion), kind=kOutput, calls=%fused_computation.25 | convolution fusion | flops 1075314688 | bytes 4194816 | tf_op jit(solution)/shard_map/dot_general | solution.py:184
  16.2 3.1 %multiply_convert_fusion.1 = (bf16[512,1024]{1,0:T(8,128)(2,1)}, f32[512,1024]{1,0:T(8,128)}) fusion(f32[1024]{0:T(1024)S(1)} %copy-done.7, f32[512]{0:T(512)S(1)} %broadcast_select_fusion, bf16[512,1024]{1,0:T(8,128)(2,1)S(1)} %select_convert_fusion.2, bf16[1024,1024]{1,0:T(8,128)(2,1)S(1)} %copy-done), kind=kOutput, calls=%fused_computation.23 | convolution fusion | flops 1077411840 | bytes 6297600 | tf_op jit(solution)/shard_map/dot_general | solution.py:186
  19.4 6.4 %all-to-all-start.1 = ((bf16[32,16,1024]{2,1,0:T(8,128)(2,1)}), bf16[32,16,1024]{2,1,0:T(8,128)(2,1)S(1)}, u32[]{:S(2)}, u32[]{:S(2)}) async-start(bf16[32,16,1024]{2,1,0:T(8,128)(2,1)} %bitcast.1), calls=%async_computation.1 | async-start | bytes 2097152 | tf_op jit(solution)/shard_map/all_to_all | solution.py:33
  25.7 3.9 %copy.40 = bf16[1024,1024]{0,1:T(8,128)(2,1)} copy(bf16[1024,1024]{1,0:T(8,128)(2,1)} %param.17) | data formatting | bytes 4194304 | tf_op args[5]
  29.7 5.3 %copy.42 = f32[1024,1024]{0,1:T(8,128)} copy(f32[1024,1024]{1,0:T(8,128)} %param.23) | data formatting | bytes 8388608 | tf_op args[11]
  35.7 16.2 %all-to-all-done.1 = bf16[32,16,1024]{2,1,0:T(8,128)(2,1)S(1)} async-done(((bf16[32,16,1024]{2,1,0:T(8,128)(2,1)}), bf16[32,16,1024]{2,1,0:T(8,128)(2,1)S(1)}, u32[]{:S(2)}, u32[]{:S(2)}) %all-to-all-start.1) | async-done | bytes 1048608 | tf_op jit(solution)/shard_map/all_to_all | solution.py:33
  52.0 1.3 divide_convert_fusion
  54.8 5.6 %multiply_reduce_fusion.1 = (f32[1024]{0:T(1024)S(1)}, f32[1024,1024]{0,1:T(8,128)S(1)}) fusion(f32[1024]{0:T(1024)S(1)} %copy-done.6, bf16[2048,1024]{1,0:T(8,128)(2,1)S(1)} %copy-done.8, bf16[1024,1024]{0,1:T(8,128)(2,1)S(1)} %divide_convert_fusion, bf16[1024,1024]{0,1:T(8,128)(2,1)S(1)} %copy-done.4), kind=kOutput, calls=%fused_computation.6 | convolution fusion | flops 4310694912 | bytes 12591104 | tf_op jit(solution)/shard_map/dot_general | solution.py:204
  60.5 1.8 multiply_reduce_fusion
  62.3 4.6 %convert_reduce_fusion = (f32[1024]{0:T(1024)S(1)}, bf16[1024,1024]{0,1:T(8,128)(2,1)S(1)}, f32[1024,1024]{0,1:T(8,128)}) fusion(f32[1024,1024]{0,1:T(8,128)S(1)} %copy-done.2, f32[1024]{0:T(1024)S(1)} %multiply_reduce_fusion, f32[1024,1024]{0,1:T(8,128)S(1)} %get-tuple-element.56, f32[1024]{0:T(1024)S(1)} %copy-done.6, f32[1024]{0:T(1024)S(1)} %add_rsqrt_fusion), kind=kLoop, calls=%fused_computation.3 | loop fusion | flops 17824768 | bytes 14696448 | tf_op jit(solution)/shard_map/reduce_sum | solution.py:213
  66.9 1.3 copy-done.5
  68.2 4.6 %fusion.16 = f32[1024,2048]{1,0:T(8,128)S(1)} fusion(bf16[1024,1024]{0,1:T(8,128)(2,1)S(1)} %get-tuple-element.43, bf16[2048,1024]{1,0:T(8,128)(2,1)S(1)} %copy-done.8), kind=kOutput, calls=%fused_computation.51 | convolution fusion | flops 4294967296 | bytes 14680064 | tf_op jit(solution)/shard_map/dot_general | solution.py:15
  72.8 4.2 %fusion.15 = (f32[1024,1024]{1,0:T(8,128)}, f32[1024,1024]{1,0:T(8,128)}) fusion(f32[1024,2048]{1,0:T(8,128)S(1)} %fusion.16), kind=kLoop, calls=%fused_computation.50 | loop fusion | bytes 16777216 | tf_op jit(solution)/shard_map/slice | solution.py:215
  77.0 5.3 %copy.46 = f32[1024,1024]{0,1:T(8,128)} copy(f32[1024,1024]{1,0:T(8,128)} %get-tuple-element.49) | data formatting | bytes 8388608
  82.4 4.1 %broadcast_divide_fusion = bf16[1024,1024]{0,1:T(8,128)(2,1)} fusion(f32[1024,1024]{0,1:T(8,128)} %copy.46, f32[1024]{0:T(1024)S(1)} %broadcast_maximum_fusion), kind=kLoop, calls=%fused_computation.21 | loop fusion | flops 2097152 | bytes 6295552 | tf_op jit(solution)/shard_map/div | solution.py:216
  86.5 3.9 %copy.44 = bf16[1024,1024]{1,0:T(8,128)(2,1)} copy(bf16[1024,1024]{0,1:T(8,128)(2,1)} %broadcast_divide_fusion) | data formatting | bytes 4194304 | tf_op jit(solution)/shard_map/div | solution.py:216
  90.4 4.6 %gather_fusion = bf16[512,1024]{1,0:T(8,128)(2,1)S(1)} fusion(bf16[1024,1024]{1,0:T(8,128)(2,1)} %copy.44, s32[1024]{0:T(1024)S(1)} %pad_clamp_fusion), kind=kCustom, calls=%fused_computation | custom fusion | bytes 2099200 | tf_op jit(solution)/shard_map/jit(_take)/gather | solution.py:217
  96.2 3.8 %all-to-all-start.2 = ((bf16[32,16,1024]{2,1,0:T(8,128)(2,1)}), bf16[32,16,1024]{2,1,0:T(8,128)(2,1)S(1)}, u32[]{:S(2)}, u32[]{:S(2)}) async-start(bf16[32,16,1024]{2,1,0:T(8,128)(2,1)} %select_convert_fusion.1), calls=%async_computation.2 | async-start | bytes 2097152 | tf_op jit(solution)/shard_map/all_to_all | solution.py:33
  100.1 5.3 %copy.45 = f32[1024,1024]{1,0:T(8,128)} copy(f32[1024,1024]{0,1:T(8,128)} %get-tuple-element.50) | data formatting | bytes 8388608
  105.4 9.4 %convolution_convert_fusion = bf16[2048,1024]{1,0:T(8,128)(2,1)} fusion(bf16[1024,1024]{0,1:T(8,128)(2,1)} %copy-done.5, bf16[1024,1024]{0,1:T(8,128)(2,1)} %copy-done.13, bf16[1024,1024]{0,1:T(8,128)(2,1)} %copy.40), kind=kOutput, calls=%fused_computation.10 | convolution fusion | flops 4305453056 | bytes 10485760 | tf_op jit(solution)/shard_map/dot_general | solution.py:21
  114.8 11.4 %all-to-all-done.2 = bf16[32,16,1024]{2,1,0:T(8,128)(2,1)S(1)} async-done(((bf16[32,16,1024]{2,1,0:T(8,128)(2,1)}), bf16[32,16,1024]{2,1,0:T(8,128)(2,1)S(1)}, u32[]{:S(2)}, u32[]{:S(2)}) %all-to-all-start.2) | async-done | bytes 1048608 | tf_op jit(solution)/shard_map/all_to_all | solution.py:33
  126.3 2.7 convert_reduce_fusion.1
  129.0 1.3 convolution_convert_fusion.1
  130.3 1.3 fusion.17
  131.9 2.3 add_convert_fusion
  134.2 1.4 convert_bitcast_fusion
  136.4 4.1 %pad_maximum_fusion.part_ref = bf16[4096,1024]{1,0:T(8,128)(2,1)} fusion(bf16[1024,1024]{1,0:T(8,128)(2,1)S(1)} %convert_bitcast_fusion, bf16[1024,1024]{1,0:T(8,128)(2,1)S(1)} %convolution_convert_fusion.1, bf16[2048,1024]{1,0:T(8,128)(2,1)S(1)} %copy-done.3), kind=kLoop, calls=%fused_computation.1 | loop fusion | flops 25165824 | bytes 16777216 | tf_op jit(solution)/shard_map/concatenate | solution.py:229
  140.5 100.0 %weight_gradient_sum.1 = bf16[4096,1024]{1,0:T(8,128)(2,1)} custom-call(bf16[4096,1024]{1,0:T(8,128)(2,1)} %pad_maximum_fusion.part_ref), custom_call_target="tpu_custom_call" | custom-call | tf_op jit(solution)/shard_map/weight_gradient_sum/pallas_call | solution.py:138
  240.5 6.8 %slice.36 = f32[2048,1024]{1,0:T(8,128)} slice(bf16[4096,1024]{1,0:T(8,128)(2,1)} %weight_gradient_sum.1), slice={[0:2048], [0:1024]} | slice | bytes 16777216 | tf_op jit(solution)/shard_map/slice | solution.py:241
  247.3 4.4 %fusion.14 = (f32[1024,1024]{1,0:T(8,128)}, f32[1024,1024]{1,0:T(8,128)}) fusion(bf16[4096,1024]{1,0:T(8,128)(2,1)S(1)} %copy-done.1), kind=kLoop, calls=%fused_computation.49 | loop fusion | bytes 16777216 | tf_op jit(solution)/shard_map/slice | solution.py:239
  251.7 37.7 %all-reduce = (f32[1024]{0:T(1024)}, f32[1024]{0:T(1024)}) all-reduce(f32[1024]{0:T(1024)S(1)} %get-tuple-element.44, f32[1024]{0:T(1024)S(1)} %get-tuple-element.42), channel_id=1, replica_groups=mesh['hop'=16,'par'=2] {'hop','par'}, use_global_device_ids=true, to_apply=%region_4.5 | all-reduce | flops 2048 | bytes 16384 | tf_op jit(solution)/shard_map/psum | solution.py:232
  (49 shorter events, 9.4 us)
Async XLA Ops:
  0.6 15.6 %copy-start = (bf16[1024,1024]{1,0:T(8,128)(2,1)S(1)}, bf16[1024,1024]{1,0:T(8,128)(2,1)}, u32[]{:S(2)}) copy-start(bf16[1024,1024]{1,0:T(8,128)(2,1)} %param.19) | copy-start | bytes 6291460
  3.8 15.6 %all-to-all-start = ((f32[2,32,16]{2,0,1:T(2,128)}), f32[2,32,16]{2,0,1:T(2,128)S(1)}, u32[]{:S(2)}, u32[]{:S(2)}) async-start(f32[2,32,16]{2,0,1:T(2,128)} %copy.39), calls=%async_computation | async-start | bytes 65536 | tf_op jit(solution)/shard_map/all_to_all | solution.py:191
  11.8 4.4 %copy-start.7 = (f32[1024]{0:T(1024)S(1)}, f32[1024]{0:T(1024)}, u32[]{:S(2)}) copy-start(f32[1024]{0:T(1024)} %param.20) | copy-start | bytes 12292
  15.2 1.0 copy-start.11
  19.4 32.6 %all-to-all-start.1 = ((bf16[32,16,1024]{2,1,0:T(8,128)(2,1)}), bf16[32,16,1024]{2,1,0:T(8,128)(2,1)S(1)}, u32[]{:S(2)}, u32[]{:S(2)}) async-start(bf16[32,16,1024]{2,1,0:T(8,128)(2,1)} %bitcast.1), calls=%async_computation.1 | async-start | bytes 2097152 | tf_op jit(solution)/shard_map/all_to_all | solution.py:33
  52.0 1.6 copy-start.4
  52.0 1.6 copy-start.6
  52.0 2.8 copy-start.8
  54.8 5.6 %copy-start.13 = (bf16[1024,1024]{0,1:T(8,128)(2,1)}, bf16[1024,1024]{0,1:T(8,128)(2,1)S(1)}, u32[]{:S(2)}) copy-start(bf16[1024,1024]{0,1:T(8,128)(2,1)S(1)} %divide_convert_fusion) | copy-start | bytes 6291460
  54.8 5.6 %copy-start.2 = (f32[1024,1024]{0,1:T(8,128)S(1)}, f32[1024,1024]{0,1:T(8,128)}, u32[]{:S(2)}) copy-start(f32[1024,1024]{0,1:T(8,128)} %copy.42) | copy-start | bytes 12582916
  66.9 1.3 copy-start.5
  96.2 30.1 %all-to-all-start.2 = ((bf16[32,16,1024]{2,1,0:T(8,128)(2,1)}), bf16[32,16,1024]{2,1,0:T(8,128)(2,1)S(1)}, u32[]{:S(2)}, u32[]{:S(2)}) async-start(bf16[32,16,1024]{2,1,0:T(8,128)(2,1)} %select_convert_fusion.1), calls=%async_computation.2 | async-start | bytes 2097152 | tf_op jit(solution)/shard_map/all_to_all | solution.py:33
  126.3 2.7 copy-start.12
  130.3 1.6 copy-start.9
  131.9 2.3 copy-start.10
  134.2 2.2 copy-start.3
  240.5 6.8 %copy-start.1 = (bf16[4096,1024]{1,0:T(8,128)(2,1)S(1)}, bf16[4096,1024]{1,0:T(8,128)(2,1)}, u32[]{:S(2)}) copy-start(bf16[4096,1024]{1,0:T(8,128)(2,1)} %weight_gradient_sum.1) | copy-start | bytes 25165828

commit v2 on v1

--- a/solution.py
+++ b/solution.py
@@ -155,7 +155,7 @@
     )(part)
 
 
-def body(
+def plain_body(
     child_feats,
     board_mask,
     importance,
@@ -243,11 +243,708 @@
     )
 
 
+TILE = 256
+BLOCK = 16
+
+
+def columns(index, width=TILE):
+    return pl.ds(pl.multiple_of(index * width, width), width)
+
+
+def mm(left, right):
+    return jnp.dot(left, right, preferred_element_type=jnp.float32)
+
+
+def sigmoid(value):
+    return 0.5 * jnp.tanh(0.5 * value) + 0.5
+
+
+def spread(column, width):
+    return jnp.concatenate([column] * (width // column.shape[1]), axis=1)
+
+
+class Sums:
+    def __init__(self, hop, core, groups, held, inbox, total, sems):
+        self.hop, self.core, self.groups = hop, core, groups
+        self.held, self.inbox, self.total = held, inbox, total
+        self.send, self.recv, self.out, self.into, self.own = sems
+        self.start = [jnp.int32(first) for first, _, _ in groups]
+        self.kept, self.down, self.up, self.local = {}, {}, {}, {}
+        self.levels = len(groups[0][2])
+
+    def halve(self, group, level):
+        first, rows, order = self.groups[group]
+        bit, half = order[level], rows >> (level + 1)
+        mine = own_bit(self.hop, self.core, bit)
+        away = pl.multiple_of(self.start[group] + (1 - mine) * half, half)
+        place = first + rows - (rows >> level)
+        copy = pltpu.make_async_remote_copy(
+            src_ref=self.held.at[pl.ds(away, half)],
+            dst_ref=self.inbox.at[pl.ds(place, half)],
+            send_sem=self.send.at[group, level],
+            recv_sem=self.recv.at[group, level],
+            device_id=partner(self.hop, self.core, bit),
+            device_id_type=MESH,
+        )
+        copy.start()
+        self.down[group, level] = copy
+        self.start[group] = self.start[group] + mine * half
+        self.kept[group, level] = self.start[group]
+
+    def fold(self, group, level):
+        first, rows, _ = self.groups[group]
+        half = rows >> (level + 1)
+        part = pl.ds(pl.multiple_of(self.kept[group, level], half), half)
+        place = first + rows - (rows >> level)
+        self.down[group, level].wait_recv()
+        self.held[part] = self.held[part] + self.inbox[pl.ds(place, half)]
+        if level < self.levels - 1:
+            self.halve(group, level + 1)
+        else:
+            copy = pltpu.make_async_copy(self.held.at[part], self.total.at[part], self.own.at[group])
+            copy.start()
+            self.local[group] = copy
+            self.double(group, level, self.held)
+
+    def double(self, group, level, source):
+        _, rows, order = self.groups[group]
+        half = rows >> (level + 1)
+        part = pl.ds(pl.multiple_of(self.kept[group, level], half), half)
+        copy = pltpu.make_async_remote_copy(
+            src_ref=source.at[part],
+            dst_ref=self.total.at[part],
+            send_sem=self.out.at[group, level],
+            recv_sem=self.into.at[group, level],
+            device_id=partner(self.hop, self.core, order[level]),
+            device_id_type=MESH,
+        )
+        copy.start()
+        self.up[group, level] = copy
+
+    def gather(self, group, level):
+        if level == self.levels - 1:
+            self.local[group].wait()
+        self.up[group, level].wait_recv()
+        if level > 0:
+            self.double(group, level - 1, self.total)
+
+    def finish(self):
+        for group in range(len(self.groups)):
+            for level in range(self.levels):
+                self.down[group, level].wait_send()
+                self.up[group, level].wait_send()
+
+
+def layer_kernel(
+    groups,
+    child_in,
+    importance,
+    board,
+    slot,
+    counts,
+    parent_in,
+    proj_in,
+    q_in,
+    q_bias,
+    w_in,
+    w_bias,
+    cot_in,
+    emb_out,
+    child_out,
+    parent_out,
+    total,
+    bias_out,
+    child,
+    proj,
+    q,
+    w,
+    parent,
+    cot,
+    merged,
+    scaled_slope,
+    message,
+    arrived,
+    moved,
+    pre,
+    table,
+    table_rows,
+    grad_pre,
+    grad_moved,
+    back_out,
+    back_in,
+    child_t,
+    merged_t,
+    parent_t,
+    held,
+    inbox,
+    emb,
+    weight_col,
+    board_col,
+    shrink,
+    slot_shrink,
+    got_weight,
+    got_slot,
+    info_out,
+    info_in,
+    bias_held,
+    bias_in,
+    load_sem,
+    store_sem,
+    info_sem,
+    msg_sem,
+    back_sem,
+    bias_sem,
+    sum_send,
+    sum_recv,
+    sum_out,
+    sum_in,
+    sum_own,
+):
+    hop, core = lax.axis_index("hop"), lax.axis_index("par")
+    me = hop * 2 + core
+    slots, width = child.shape
+    parents = parent.shape[0]
+    devices = counts.shape[1]
+    cap = slots // devices
+    half = slots // 2
+    levels = len(groups[0][2])
+    tiles = width // TILE
+    upper = own_bit(hop, core, levels - 2)
+    sides = (1 - upper, upper)
+    f32, bf16 = jnp.float32, jnp.bfloat16
+
+    def target(rel):
+        to_hop = hop
+        for bit in range(levels - 1):
+            if (rel >> (bit + 1)) & 1:
+                to_hop = to_hop + (1 - 2 * own_bit(hop, core, bit)) * (1 << bit)
+        to_core = 1 - core if rel & 1 else core
+        return to_hop, to_core
+
+    def rows_of(device):
+        return pl.ds(pl.multiple_of(device * cap, cap), cap)
+
+    def side_rows(side):
+        return pl.ds(pl.multiple_of(side * half, half), half)
+
+    loads = []
+    for index, (source, place) in enumerate(
+        ((child_in, child), (proj_in, proj), (q_in, q), (parent_in, parent), (w_in, w), (cot_in, cot))
+    ):
+        copy = pltpu.make_async_copy(source, place, load_sem.at[index])
+        copy.start()
+        loads.append(copy)
+
+    barrier = pltpu.get_barrier_semaphore()
+    for rel in range(1, devices):
+        pl.semaphore_signal(barrier, inc=1, device_id=target(rel), device_id_type=MESH)
+
+    lane = lax.broadcasted_iota(jnp.int32, (128, 128), 1)
+    down = lax.broadcasted_iota(jnp.int32, (128, 128), 0)
+    eye = lane == down
+    place = lax.rem(down, cap)
+
+    def column(row):
+        return jnp.sum(jnp.where(eye, jnp.broadcast_to(row, (128, 128)), 0.0), axis=1, keepdims=True)
+
+    count_row = counts[...].astype(f32)
+    for part in range(slots // 128):
+        owner = lax.broadcasted_iota(jnp.int32, (128, devices), 0) // cap + part * (128 // cap)
+        is_owner = owner == lax.broadcasted_iota(jnp.int32, (128, devices), 1)
+        live = jnp.sum(
+            jnp.where(is_owner, jnp.broadcast_to(count_row, (128, devices)), 0.0), axis=1, keepdims=True
+        )
+        weight = jnp.broadcast_to(column(importance[part : part + 1, :]), (128, 128))
+        weight = jnp.where(place.astype(f32) < live, weight, 0.0)
+        slot_at = jnp.broadcast_to(column(slot[part : part + 1, :].astype(f32)), (128, 128))
+        at = slice(part * 128, (part + 1) * 128)
+        weight_col[at, :] = weight
+        board_col[at, :] = jnp.broadcast_to(column(board[part : part + 1, :].astype(f32)), (128, 128))
+        info = jnp.where(lane == place, weight, 0.0) + jnp.where(lane == place + cap, slot_at, 0.0)
+        for owner_at in range(128 // cap):
+            info_out[part * (128 // cap) + owner_at] = jnp.sum(
+                info[owner_at * cap : (owner_at + 1) * cap, :], axis=0, keepdims=True
+            )
+
+    pl.semaphore_wait(barrier, devices - 1)
+
+    for rel in range(devices - 1, 0, -1):
+        to_hop, to_core = target(rel)
+        pltpu.make_async_remote_copy(
+            src_ref=info_out.at[to_hop * 2 + to_core],
+            dst_ref=info_in.at[me],
+            send_sem=info_sem.at[0],
+            recv_sem=info_sem.at[1],
+            device_id=(to_hop, to_core),
+            device_id_type=MESH,
+        ).start()
+    pltpu.make_async_copy(info_out.at[me], info_in.at[me], info_sem.at[1]).start()
+
+    def send_side(source, place_ref, sem, side_index):
+        first = devices // 2 if side_index == 0 else 0
+        rels = sorted(range(first, first + devices // 2), key=lambda rel: (rel & 1, -rel))
+        for rel in rels:
+            if rel == 0:
+                pltpu.make_async_copy(
+                    source.at[rows_of(me)], place_ref.at[rows_of(me)], sem.at[1, side_index]
+                ).start()
+                continue
+            to_hop, to_core = target(rel)
+            pltpu.make_async_remote_copy(
+                src_ref=source.at[rows_of(to_hop * 2 + to_core)],
+                dst_ref=place_ref.at[rows_of(me)],
+                send_sem=sem.at[0, side_index],
+                recv_sem=sem.at[1, side_index],
+                device_id=(to_hop, to_core),
+                device_id_type=MESH,
+            ).start()
+
+    def wait_side(place_ref, sem, side_index):
+        rows = side_rows(sides[side_index])
+        pltpu.make_async_copy(place_ref.at[rows], place_ref.at[rows], sem.at[1, side_index]).wait()
+
+    def wait_sent(source, sem):
+        for side_index, rows in ((0, half), (1, half - cap)):
+            part = source.at[pl.ds(0, rows)]
+            pltpu.make_async_copy(part, part, sem.at[0, side_index]).wait()
+
+    loads[0].wait()
+    loads[1].wait()
+    for side_index, side in enumerate(sides):
+        rows = side_rows(side)
+        boards = spread(board_col[rows, :], TILE) == 1.0
+
+        @pl.loop(0, tiles)
+        def _(tile):
+            projected = mm(child[rows, :], proj[:, columns(tile)])
+            raw = child[rows, columns(tile)]
+            merged[rows, columns(tile)] = jnp.where(boards, projected, raw.astype(f32)).astype(bf16)
+
+        if side_index == 0:
+            loads[2].wait()
+        weights = spread(weight_col[rows, :], TILE)
+
+        @pl.loop(0, tiles)
+        def _(tile):
+            value = mm(merged[rows, :], q[:, columns(tile)]) + q_bias[:, columns(tile)]
+            gate = sigmoid(value)
+            act = value * gate
+            message[rows, columns(tile)] = (weights * act).astype(bf16)
+            scaled_slope[rows, columns(tile)] = weights * (gate + act * (1.0 - gate))
+
+        send_side(message, arrived, msg_sem, side_index)
+
+    loads[3].wait()
+    loads[4].wait()
+
+    @pl.loop(0, tiles)
+    def _(tile):
+        @pl.loop(0, parents // 512)
+        def _(block):
+            pre[columns(block, 512), columns(tile)] = (
+                mm(parent[columns(block, 512), :], w[pl.ds(0, width), columns(tile)])
+                + w_bias[:, columns(tile)]
+            )
+
+    info_all = pltpu.make_async_copy(info_in, info_in, info_sem.at[1])
+    info_all.wait()
+    lane16 = lax.broadcasted_iota(jnp.int32, (cap, 128), 1)
+    down16 = lax.broadcasted_iota(jnp.int32, (cap, 128), 0)
+    for device in range(devices):
+        got = jnp.broadcast_to(info_in[device], (cap, 128))
+        at = slice(device * cap, (device + 1) * cap)
+        got_weight[at, :] = jnp.broadcast_to(
+            jnp.sum(jnp.where(lane16 == down16, got, 0.0), axis=1, keepdims=True), (cap, 128)
+        )
+        got_slot[at, :] = jnp.broadcast_to(
+            jnp.sum(jnp.where(lane16 == down16 + cap, got, 0.0), axis=1, keepdims=True), (cap, 128)
+        )
+
+    for part in range(parents // 128):
+        want = (lax.broadcasted_iota(jnp.int32, (128, 128), 1) + part * 128).astype(f32)
+        weight_sum = jnp.zeros((1, 128), f32)
+        for block in range(slots // 128):
+            at = slice(block * 128, (block + 1) * 128)
+            hit = got_slot[at, :] == want
+            table_rows[at, part * 128 : (part + 1) * 128] = jnp.where(hit, 1.0, 0.0).astype(bf16)
+            weight_sum = weight_sum + jnp.sum(jnp.where(hit, got_weight[at, :], 0.0), axis=0, keepdims=True)
+        inverse = 1.0 / jnp.maximum(weight_sum, 1.0)
+        shrink[part * 128 : (part + 1) * 128, :] = jnp.broadcast_to(column(inverse), (128, 128))
+        for block in range(slots // 128):
+            at = slice(block * 128, (block + 1) * 128)
+            hit = got_slot[at, :] == want
+            term = jnp.where(hit, jnp.broadcast_to(inverse, (128, 128)), 0.0)
+            if part == 0:
+                slot_shrink[at, :] = term
+            else:
+                slot_shrink[at, :] = slot_shrink[at, :] + term
+    for block in range(slots // 128):
+        at = slice(block * 128, (block + 1) * 128)
+        slot_shrink[at, :] = jnp.broadcast_to(
+            jnp.sum(slot_shrink[at, :], axis=1, keepdims=True), (128, 128)
+        )
+
+    def transpose_into(place_ref, source, blocks):
+        for block in range(blocks):
+
+            @pl.loop(0, source.shape[1] // TILE)
+            def _(tile):
+                part = source[block * TILE : (block + 1) * TILE, columns(tile)]
+                place_ref[block, columns(tile), :] = part.T
+
+    transpose_into(table, table_rows, slots // TILE)
+    transpose_into(child_t, child, slots // TILE)
+    transpose_into(merged_t, merged, slots // TILE)
+    transpose_into(parent_t, parent, parents // TILE)
+
+    def add_messages(side_index):
+        side = sides[side_index]
+        rows = side_rows(side)
+
+        @pl.loop(0, tiles)
+        def _(tile):
+            moved[rows, columns(tile)] = mm(arrived[rows, :], w[pl.ds(width, width), columns(tile)]).astype(bf16)
+
+        @pl.loop(0, tiles)
+        def _(tile):
+            @pl.loop(0, parents // 512)
+            def _(block):
+                at = columns(block, 512)
+                pre[at, columns(tile)] = pre[at, columns(tile)] + spread(shrink[at, :], TILE) * mm(
+                    table[side, at, :], moved[rows, columns(tile)]
+                )
+
+    wait_side(arrived, msg_sem, 1)
+    add_messages(1)
+    loads[5].wait()
+    wait_side(arrived, msg_sem, 0)
+    add_messages(0)
+
+    @pl.loop(0, parents // BLOCK)
+    def _(block):
+        at = columns(block, BLOCK)
+        value = pre[at, :]
+        turn = cot[at, :]
+        gate = sigmoid(value)
+        act = value * gate
+        inv = lax.rsqrt(jnp.sum(act * act, axis=1, keepdims=True) + 1e-06)
+        share = jnp.sum(turn * act, axis=1, keepdims=True) * (inv * inv * inv)
+        emb[at, :] = (act * inv).astype(bf16)
+        grad_pre[at, :] = ((turn * inv - act * share) * (gate + act * (1.0 - gate))).astype(bf16)
+
+    stores = [pltpu.make_async_copy(emb, emb_out, store_sem.at[0])]
+    stores[0].start()
+
+    for side_index, side in enumerate(sides):
+        rows = side_rows(side)
+        shrinks = spread(slot_shrink[rows, :], TILE)
+
+        @pl.loop(0, tiles)
+        def _(tile):
+            grad_moved[rows, columns(tile)] = (
+                shrinks * mm(table_rows[rows, :], grad_pre[:, columns(tile)])
+            ).astype(bf16)
+
+        @pl.loop(0, tiles)
+        def _(tile):
+            turned = w[pl.ds(pl.multiple_of(width + tile * TILE, TILE), TILE), :]
+            back_out[rows, columns(tile)] = times_transpose(grad_moved[rows, :], turned).astype(bf16)
+
+        send_side(back_out, back_in, back_sem, side_index)
+
+    sums = Sums(hop, core, groups, held, inbox, total, (sum_send, sum_recv, sum_out, sum_in, sum_own))
+    w_groups = [g for g, (first, _, _) in enumerate(groups) if first < 2 * width]
+    q_groups = [g for g, (first, _, _) in enumerate(groups) if 2 * width <= first < 3 * width]
+    p_groups = [g for g, (first, _, _) in enumerate(groups) if first >= 3 * width]
+
+    @pl.loop(0, tiles)
+    def _(tile):
+        @pl.loop(0, tiles)
+        def _(block):
+            total_part = jnp.zeros((TILE, TILE), f32)
+            for part in range(parents // TILE):
+                total_part = total_part + mm(
+                    parent_t[part, columns(block), :],
+                    grad_pre[part * TILE : (part + 1) * TILE, columns(tile)],
+                )
+            held[columns(block), columns(tile)] = total_part.astype(bf16)
+
+    for group in w_groups[: len(w_groups) // 2]:
+        sums.halve(group, 0)
+    transpose_into(table, arrived, slots // TILE)
+
+    @pl.loop(0, tiles)
+    def _(tile):
+        @pl.loop(0, tiles)
+        def _(block):
+            total_part = jnp.zeros((TILE, TILE), f32)
+            for part in range(slots // TILE):
+                total_part = total_part + mm(
+                    table[part, columns(block), :],
+                    grad_moved[part * TILE : (part + 1) * TILE, columns(tile)],
+                )
+            at = pl.ds(pl.multiple_of(width + block * TILE, TILE), TILE)
+            held[at, columns(tile)] = total_part.astype(bf16)
+
+    for group in w_groups[len(w_groups) // 2 :]:
+        sums.halve(group, 0)
+    bias_held[0] = jnp.zeros(bias_held.shape[1:], f32)
+    bias_held[0, 0:1, :] = mm(jnp.ones((16, parents), bf16), grad_pre[...])[0:1, :]
+
+    for group in w_groups:
+        sums.fold(group, 0)
+
+    @pl.loop(0, tiles)
+    def _(tile):
+        @pl.loop(0, parents // 512)
+        def _(block):
+            parent[columns(block, 512), columns(tile)] = times_transpose(
+                grad_pre[columns(block, 512), :], w[columns(tile), :]
+            ).astype(bf16)
+
+    stores.append(pltpu.make_async_copy(parent, parent_out, store_sem.at[1]))
+    stores[1].start()
+    wait_sent(message, msg_sem)
+
+    def child_front(side_index):
+        rows = side_rows(sides[side_index])
+
+        @pl.loop(0, tiles)
+        def _(tile):
+            grad_moved[rows, columns(tile)] = (
+                scaled_slope[rows, columns(tile)] * back_in[rows, columns(tile)].astype(f32)
+            ).astype(bf16)
+
+    def weight_sums(side_index, turned, grads, partial, base):
+        side = sides[side_index]
+        rows = side_rows(side)
+
+        @pl.loop(0, tiles)
+        def _(tile):
+            @pl.loop(0, width // 512)
+            def _(block):
+                at = columns(block, 512)
+                value = mm(turned[side, at, :], grads[rows, columns(tile)])
+                if side_index == 1:
+                    partial[at, columns(tile)] = value
+                else:
+                    place_at = pl.ds(pl.multiple_of(base + block * 512, 512), 512)
+                    held[place_at, columns(tile)] = (value + partial[at, columns(tile)]).astype(bf16)
+
+    def child_middle(side_index):
+        rows = side_rows(sides[side_index])
+        boards = spread(board_col[rows, :], TILE) == 1.0
+
+        @pl.loop(0, tiles)
+        def _(tile):
+            value = times_transpose(grad_moved[rows, :], q[columns(tile), :])
+            moved[rows, columns(tile)] = jnp.where(boards, value, 0.0).astype(bf16)
+            scaled_slope[rows, columns(tile)] = jnp.where(boards, 0.0, value)
+
+    def child_end(side_index):
+        rows = side_rows(sides[side_index])
+
+        @pl.loop(0, tiles)
+        def _(tile):
+            value = times_transpose(moved[rows, :], proj[columns(tile), :])
+            message[rows, columns(tile)] = (scaled_slope[rows, columns(tile)] + value).astype(bf16)
+
+    wait_side(back_in, back_sem, 1)
+    child_front(1)
+    weight_sums(1, merged_t, grad_moved, pre, 2 * width)
+    child_middle(1)
+    weight_sums(1, child_t, moved, cot, 3 * width)
+    child_end(1)
+
+    for group in w_groups:
+        sums.fold(group, 1)
+
+    wait_side(back_in, back_sem, 0)
+    child_front(0)
+    weight_sums(0, merged_t, grad_moved, pre, 2 * width)
+    for group in q_groups:
+        sums.halve(group, 0)
+    child_middle(0)
+    weight_sums(0, child_t, moved, cot, 3 * width)
+    for group in p_groups:
+        sums.halve(group, 0)
+
+    bias_held[0, 1:2, :] = mm(jnp.ones((16, slots), bf16), grad_moved[...])[0:1, :]
+    bias_copies = []
+
+    def send_bias(level):
+        copy = pltpu.make_async_remote_copy(
+            src_ref=bias_held.at[level],
+            dst_ref=bias_in.at[level],
+            send_sem=bias_sem.at[0, level],
+            recv_sem=bias_sem.at[1, level],
+            device_id=partner(hop, core, groups[0][2][level]),
+            device_id_type=MESH,
+        )
+        copy.start()
+        bias_copies.append(copy)
+
+    def fold_bias(level):
+        bias_copies[level].wait_recv()
+        both = bias_held[level] + bias_in[level]
+        if level < levels - 1:
+            bias_held[level + 1] = both
+            send_bias(level + 1)
+        else:
+            bias_out[...] = both
+
+    send_bias(0)
+    child_end(0)
+    stores.append(pltpu.make_async_copy(message, child_out, store_sem.at[2]))
+    stores[2].start()
+
+    late = q_groups + p_groups
+    plan = [("late", 0), ("w", 2), ("late", 1), ("w", 3), ("late", 2), ("w", 4), ("late", 3), ("w_up", 4)]
+    plan += [("late", 4), ("w_up", 3), ("late_up", 4), ("w_up", 2), ("late_up", 3), ("w_up", 1)]
+    plan += [("late_up", 2), ("w_up", 0), ("late_up", 1), ("late_up", 0)]
+    for what, level in plan:
+        for group in w_groups if what[0] == "w" else late:
+            (sums.gather if what.endswith("up") else sums.fold)(group, level)
+        if what == "late":
+            fold_bias(level)
+
+    sums.finish()
+    for copy in bias_copies:
+        copy.wait_send()
+    wait_sent(back_out, back_sem)
+    sent = info_out.at[pl.ds(0, devices - 1)]
+    pltpu.make_async_copy(sent, sent, info_sem.at[0]).wait()
+    for copy in stores:
+        copy.wait()
+
+
+def sum_groups(width):
+    x, y, z0, z1 = range(4)
+    orders = [[x, y, z0, z1], [y, x, z0, z1], [x, z0, y, z1], [y, z0, x, z1]]
+    orders += [[x, y, z0, z1], [y, x, z0, z1], [z0, x, y, z1], [z0, y, x, z1]]
+    rows = 4 * width // len(orders)
+    return [(index * rows, rows, [CORE] + order) for index, order in enumerate(orders)]
+
+
+def fused_body(
+    child_feats,
+    board_mask,
+    importance,
+    parent_slot,
+    send_counts,
+    parent_feats,
+    proj_weight,
+    q_weight,
+    q_bias,
+    w_weight,
+    w_bias,
+    emb_cotangent,
+):
+    slots, width = child_feats.shape
+    parents = parent_feats.shape[0]
+    devices = send_counts.shape[1]
+    groups = sum_groups(width)
+    levels = len(groups[0][2])
+    f32, bf16 = jnp.float32, jnp.bfloat16
+    half = slots // 2
+    vmem = pl.BlockSpec(memory_space=pltpu.VMEM)
+    hbm = pl.BlockSpec(memory_space=pl.ANY)
+    dma = pltpu.SemaphoreType.DMA
+    shape = jax.ShapeDtypeStruct
+    emb, grad_child, grad_parent, total, biases = pl.pallas_call(
+        functools.partial(layer_kernel, groups),
+        name="layer",
+        out_shape=(
+            shape((parents, width), bf16),
+            shape((slots, width), bf16),
+            shape((parents, width), bf16),
+            shape((4 * width, width), bf16),
+            shape((8, width), f32),
+        ),
+        in_specs=[hbm, vmem, vmem, vmem, vmem, hbm, hbm, hbm, vmem, hbm, vmem, hbm],
+        out_specs=(hbm, hbm, hbm, hbm, vmem),
+        scratch_shapes=[
+            pltpu.VMEM((slots, width), bf16),
+            pltpu.VMEM((width, width), bf16),
+            pltpu.VMEM((width, width), bf16),
+            pltpu.VMEM((2 * width, width), bf16),
+            pltpu.VMEM((parents, width), bf16),
+            pltpu.VMEM((parents, width), f32),
+            pltpu.VMEM((slots, width), bf16),
+            pltpu.VMEM((slots, width), f32),
+            pltpu.VMEM((slots, width), bf16),
+            pltpu.VMEM((slots, width), bf16),
+            pltpu.VMEM((slots, width), bf16),
+            pltpu.VMEM((parents, width), f32),
+            pltpu.VMEM((2, parents, half), bf16),
+            pltpu.VMEM((slots, parents), bf16),
+            pltpu.VMEM((parents, width), bf16),
+            pltpu.VMEM((slots, width), bf16),
+            pltpu.VMEM((slots, width), bf16),
+            pltpu.VMEM((slots, width), bf16),
+            pltpu.VMEM((2, width, half), bf16),
+            pltpu.VMEM((2, width, half), bf16),
+            pltpu.VMEM((parents // TILE, width, TILE), bf16),
+            pltpu.VMEM((4 * width, width), bf16),
+            pltpu.VMEM((4 * width, width), bf16),
+            pltpu.VMEM((parents, width), bf16),
+            pltpu.VMEM((slots, 128), f32),
+            pltpu.VMEM((slots, 128), f32),
+            pltpu.VMEM((parents, 128), f32),
+            pltpu.VMEM((slots, 128), f32),
+            pltpu.VMEM((slots, 128), f32),
+            pltpu.VMEM((slots, 128), f32),
+            pltpu.VMEM((devices, 1, 128), f32),
+            pltpu.VMEM((devices, 1, 128), f32),
+            pltpu.VMEM((levels, 8, width), f32),
+            pltpu.VMEM((levels, 8, width), f32),
+            dma((6,)),
+            dma((3,)),
+            dma((2,)),
+            dma((2, 2)),
+            dma((2, 2)),
+            dma((2, levels)),
+        ]
+        + [dma((len(groups), levels))] * 4
+        + [dma((len(groups),))],
+        compiler_params=pltpu.CompilerParams(
+            collective_id=1, has_side_effects=True, vmem_limit_bytes=62 << 20
+        ),
+        cost_estimate=pl.CostEstimate(
+            flops=36 * slots * width * width, bytes_accessed=40 << 20, transcendentals=3 * parents * width
+        ),
+    )(
+        child_feats,
+        importance.reshape(-1, 128),
+        board_mask.reshape(-1, 128),
+        parent_slot.reshape(-1, 128),
+        send_counts,
+        parent_feats,
+        proj_weight,
+        q_weight,
+        q_bias.reshape(1, -1),
+        w_weight,
+        w_bias.reshape(1, -1),
+        emb_cotangent,
+    )
+    return (
+        emb.astype(f32),
+        grad_child,
+        grad_parent.astype(f32),
+        total[3 * width :].astype(f32),
+        total[2 * width : 3 * width].astype(f32),
+        biases[1],
+        total[: 2 * width].astype(f32),
+        biases[0],
+    )
+
+
 def solution(mesh):
     rows = P(("hop", "par"), None)
     flat = P(("hop", "par"))
+    fused = mesh.shape["hop"] == 16 and mesh.shape["par"] == 2
     return jax.shard_map(
-        body,
+        fused_body if fused else plain_body,
         mesh=mesh,
         in_specs=(rows, flat, flat, flat, rows, rows, P(), P(), P(), P(), P(), rows),
         out_specs=(rows, rows, rows, P(), P(), P(), P(), P()),

time: 293 us -> 181 us (0.62)
  Pallas kernels: 100 us -> 159 us
  local copies, waits for them, and re-layouts: 50 us -> 2.51 us
  blocking collectives: 37.7 us -> 0 us
  matrix products: 33.8 us -> 0 us
  waiting for transfers between devices: 27.7 us -> 0 us
  starting transfers between devices: 17.5 us -> 0 us
  other arithmetic: 21.9 us -> 16.2 us
    pallas_call x1, Pallas kernels: 100 us -> 159 us  [fused_body(): pl.pallas_call(functools.partial(layer_kernel, groups), name='layer', out...]
    psum x1 -> x0, blocking collectives: 37.7 us -> none  [body(): grad_qbias, grad_wbias = lax.psum((grad_qbias, grad_wbias), ('hop', 'par'))]
    dot_general x10 -> x0, matrix products: 33.8 us -> none  [the longest x3 12.1 us: contract_rows(): lax.dot_general(left, right, (((0,), (0,)), ((), ())), preferred_element_...]
    all_to_all x3 -> x0, waiting for transfers between devices: 27.7 us -> none  [the longest x2 27.7 us: send_rows(): lax.all_to_all(parcel, ('hop', 'par'), split_axis=0, concat_axis=0, tiled...]
    unnamed x32 -> x9, local copies, waits for them, and re-layouts: 24.9 us -> 0.99 us
    all_to_all x3 -> x0, starting transfers between devices: 17.5 us -> none  [the longest x2 10.2 us: send_rows(): lax.all_to_all(parcel, ('hop', 'par'), split_axis=0, concat_axis=0, tiled...]
    convert_element_type x4, other arithmetic: 2.18 us -> 16.2 us  [the longest x1 6.83 us: fused_body(): total[2 * width:3 * width].astype(f32)]
    slice x3 -> x1, local copies, waits for them, and re-layouts: 15.5 us -> 1.52 us  [fused_body(): biases[0]]
  transfers between devices with their start and end apart: 3 -> 0, of which waited for: 2 -> 0; matrix products, arithmetic and copies ran while one was open for 11% -> 0% of each run, Pallas kernels for 0% -> 0%
where the time goes in v2:
time: 181 us; the launch traced here: 179 us
  Pallas kernels  159 us (88%)
  other arithmetic  16.2 us (9%)
  local copies, waits for them, and re-layouts  2.51 us (1%)
    pallas_call x1, Pallas kernels, fused_body(): pl.pallas_call(functools.partial(layer_kernel, groups), name='layer', out...  159 us
    convert_element_type x1, other arithmetic, fused_body(): total[2 * width:3 * width].astype(f32)  6.83 us
    convert_element_type x1, other arithmetic, fused_body(): total[:2 * width].astype(f32)  4.44 us

profile of v2, /device:TPU:0, one launch (start us, length us, event | category | flops | bytes accessed | tf_op | source)
XLA Modules:
  0.0 178.8 jit_solution(11520018334487799370)
XLA Ops:
  0.6 159.4 %layer.1 = (bf16[1024,1024]{1,0:T(8,128)(2,1)}, bf16[512,1024]{1,0:T(8,128)(2,1)}, bf16[1024,1024]{1,0:T(8,128)(2,1)}, bf16[4096,1024]{1,0:T(8,128)(2,1)}, f32[8,1024]{1,0:T(8,128)}) custom-call(bf16[512,1024]{1,0:T(8,128)(2,1)} %child_in.1, f32[4,128]{1,0:T(4,128)} %bitcast.11, s32[4,128]{1,0:T(4,128)} %bitcast.12, s32[4,128]{1,0:T(4,128)} %bitcast.13, ...), custom_call_target="tpu_custom_call" | custom-call | flops 19327352832 | bytes 41943040 | tf_op jit(solution)/shard_map/layer/pallas_call | solution.py:854
  160.0 0.0 copy-start
  160.0 6.8 %slice_convert_fusion.1 = (f32[1024,1024]{1,0:T(8,128)}, f32[1024,1024]{1,0:T(8,128)}) fusion(bf16[4096,1024]{1,0:T(8,128)(2,1)} %get-tuple-element.16), kind=kLoop, calls=%fused_computation.1 | loop fusion | flops 2097152 | bytes 12582912 | tf_op jit(solution)/shard_map/convert_element_type | solution.py:935
  166.9 0.0 copy-done
  166.9 0.0 copy-start.2
  166.9 4.4 %slice_convert_fusion = f32[2048,1024]{1,0:T(8,128)} fusion(bf16[4096,1024]{1,0:T(8,128)(2,1)S(1)} %copy-done), kind=kLoop, calls=%fused_computation | loop fusion | flops 2097152 | bytes 12582912 | tf_op jit(solution)/shard_map/convert_element_type | solution.py:937
  171.3 0.0 copy-start.1
  171.3 1.5 fusion
  172.8 0.0 copy-done.2
  172.8 2.5 %convert_element_type.15 = f32[1024,1024]{1,0:T(8,128)} convert(bf16[1024,1024]{1,0:T(8,128)(2,1)S(1)} %copy-done.2) | non-fusion elementwise | flops 1048576 | bytes 6291456 | tf_op jit(solution)/shard_map/convert_element_type | solution.py:931
  175.3 0.0 copy-start.3
  175.3 0.0 copy-done.1
  175.3 2.5 %convert_element_type.16 = f32[1024,1024]{1,0:T(8,128)} convert(bf16[1024,1024]{1,0:T(8,128)(2,1)S(1)} %copy-done.1) | non-fusion elementwise | flops 1048576 | bytes 6291456 | tf_op jit(solution)/shard_map/convert_element_type | solution.py:933
  177.8 0.0 copy-done.3
  177.8 1.0 copy.21
Async XLA Ops:
  160.0 6.8 %copy-start = (bf16[4096,1024]{1,0:T(8,128)(2,1)S(1)}, bf16[4096,1024]{1,0:T(8,128)(2,1)}, u32[]{:S(2)}) copy-start(bf16[4096,1024]{1,0:T(8,128)(2,1)} %get-tuple-element.16) | copy-start | bytes 25165828
  166.9 6.0 %copy-start.2 = (bf16[1024,1024]{1,0:T(8,128)(2,1)S(1)}, bf16[1024,1024]{1,0:T(8,128)(2,1)}, u32[]{:S(2)}) copy-start(bf16[1024,1024]{1,0:T(8,128)(2,1)} %get-tuple-element.13) | copy-start | bytes 6291460
  171.3 4.0 %copy-start.1 = (bf16[1024,1024]{1,0:T(8,128)(2,1)S(1)}, bf16[1024,1024]{1,0:T(8,128)(2,1)}, u32[]{:S(2)}) copy-start(bf16[1024,1024]{1,0:T(8,128)(2,1)} %get-tuple-element.15) | copy-start | bytes 6291460
  175.3 2.5 %copy-start.3 = (bf16[512,1024]{1,0:T(8,128)(2,1)S(1)}, bf16[512,1024]{1,0:T(8,128)(2,1)}, u32[]{:S(2)}) copy-start(bf16[512,1024]{1,0:T(8,128)(2,1)} %get-tuple-element.31) | copy-start | bytes 3145732

commit v3 on v2

--- a/solution.py
+++ b/solution.py
@@ -243,8 +243,8 @@
     )
 
 
-TILE = 256
-BLOCK = 16
+TILE = 512
+BLOCK = 128
 
 
 def columns(index, width=TILE):
@@ -268,71 +268,116 @@
         self.hop, self.core, self.groups = hop, core, groups
         self.held, self.inbox, self.total = held, inbox, total
         self.send, self.recv, self.out, self.into, self.own = sems
-        self.start = [jnp.int32(first) for first, _, _ in groups]
-        self.kept, self.down, self.up, self.local = {}, {}, {}, {}
         self.levels = len(groups[0][2])
-
-    def halve(self, group, level):
-        first, rows, order = self.groups[group]
-        bit, half = order[level], rows >> (level + 1)
-        mine = own_bit(self.hop, self.core, bit)
-        away = pl.multiple_of(self.start[group] + (1 - mine) * half, half)
-        place = first + rows - (rows >> level)
-        copy = pltpu.make_async_remote_copy(
-            src_ref=self.held.at[pl.ds(away, half)],
-            dst_ref=self.inbox.at[pl.ds(place, half)],
+        low, high = own_bit(hop, core, 2), own_bit(hop, core, 3)
+        self.is_inner = low != high
+        self.high = high
+        place = 0
+        self.plans = []
+        for first, rows, order in groups:
+            start, size, inner, steps = jnp.int32(first), rows, False, []
+            for kind in order:
+                if kind == "i":
+                    step = (kind, start, start, size, place, inner)
+                    inner = True
+                else:
+                    size //= 2
+                    mine = high if kind == "m" else own_bit(hop, core, "cxypq".index(kind) - 1)
+                    step = (kind, start + (1 - mine) * size, start + mine * size, size, place, inner)
+                    start = start + mine * size
+                    inner = inner or kind == "m"
+                steps.append(step)
+                place += size
+            self.plans.append(steps)
+
+    def other(self, kind):
+        if kind == "m":
+            return (self.hop + (1 - 2 * self.high) * 4, self.core)
+        return partner(self.hop, self.core, "cxypq".index(kind.replace("i", "p")) - 1)
+
+    def when(self, role, what):
+        if role is None:
+            what()
+        else:
+            pl.when(self.is_inner if role == "inner" else jnp.logical_not(self.is_inner))(what)
+
+    def roles(self, group, level, upward):
+        kind, _, _, _, _, inner = self.plans[group][level]
+        if kind == "i":
+            return ("inner", "outer") if upward else ("outer", "inner")
+        role = "inner" if inner or kind == "m" else None
+        return role, role
+
+    def rows(self, start, size):
+        return pl.ds(pl.multiple_of(start, size), size)
+
+    def down(self, group, level):
+        kind, away, _, size, place, _ = self.plans[group][level]
+        return pltpu.make_async_remote_copy(
+            src_ref=self.held.at[self.rows(away, size)],
+            dst_ref=self.inbox.at[pl.ds(place, size)],
             send_sem=self.send.at[group, level],
             recv_sem=self.recv.at[group, level],
-            device_id=partner(self.hop, self.core, bit),
+            device_id=self.other(kind),
             device_id_type=MESH,
         )
-        copy.start()
-        self.down[group, level] = copy
-        self.start[group] = self.start[group] + mine * half
-        self.kept[group, level] = self.start[group]
-
-    def fold(self, group, level):
-        first, rows, _ = self.groups[group]
-        half = rows >> (level + 1)
-        part = pl.ds(pl.multiple_of(self.kept[group, level], half), half)
-        place = first + rows - (rows >> level)
-        self.down[group, level].wait_recv()
-        self.held[part] = self.held[part] + self.inbox[pl.ds(place, half)]
-        if level < self.levels - 1:
-            self.halve(group, level + 1)
-        else:
-            copy = pltpu.make_async_copy(self.held.at[part], self.total.at[part], self.own.at[group])
-            copy.start()
-            self.local[group] = copy
-            self.double(group, level, self.held)
-
-    def double(self, group, level, source):
-        _, rows, order = self.groups[group]
-        half = rows >> (level + 1)
-        part = pl.ds(pl.multiple_of(self.kept[group, level], half), half)
-        copy = pltpu.make_async_remote_copy(
+
+    def up(self, group, level):
+        kind, _, kept, size, _, _ = self.plans[group][level]
+        source = self.held if level == self.levels - 1 else self.total
+        part = self.rows(kept, size)
+        return pltpu.make_async_remote_copy(
             src_ref=source.at[part],
             dst_ref=self.total.at[part],
             send_sem=self.out.at[group, level],
             recv_sem=self.into.at[group, level],
-            device_id=partner(self.hop, self.core, order[level]),
+            device_id=self.other(kind),
             device_id_type=MESH,
         )
-        copy.start()
-        self.up[group, level] = copy
+
+    def own_copy(self, group):
+        _, _, kept, size, _, _ = self.plans[group][-1]
+        part = self.rows(kept, size)
+        return pltpu.make_async_copy(self.held.at[part], self.total.at[part], self.own.at[group])
+
+    def halve(self, group, level):
+        self.when(self.roles(group, level, False)[0], lambda: self.down(group, level).start())
+
+    def double(self, group, level):
+        self.when(self.roles(group, level, True)[0], lambda: self.up(group, level).start())
+
+    def fold(self, group, level):
+        _, _, kept, size, place, _ = self.plans[group][level]
+
+        def add():
+            self.down(group, level).wait_recv()
+            part = self.rows(kept, size)
+            self.held[part] = self.held[part] + self.inbox[pl.ds(place, size)]
+            if level == self.levels - 1:
+                self.own_copy(group).start()
+                self.up(group, level).start()
+
+        self.when(self.roles(group, level, False)[1], add)
+        if level < self.levels - 1:
+            self.halve(group, level + 1)
 
     def gather(self, group, level):
-        if level == self.levels - 1:
-            self.local[group].wait()
-        self.up[group, level].wait_recv()
+        def take():
+            if level == self.levels - 1:
+                self.own_copy(group).wait()
+            self.up(group, level).wait_recv()
+
+        self.when(self.roles(group, level, True)[1], take)
         if level > 0:
-            self.double(group, level - 1, self.total)
+            self.double(group, level - 1)
 
     def finish(self):
         for group in range(len(self.groups)):
             for level in range(self.levels):
-                self.down[group, level].wait_send()
-                self.up[group, level].wait_send()
+                self.when(
+                    self.roles(group, level, False)[0], lambda: self.down(group, level).wait_send()
+                )
+                self.when(self.roles(group, level, True)[0], lambda: self.up(group, level).wait_send())
 
 
 def layer_kernel(
@@ -366,15 +411,11 @@
     arrived,
     moved,
     pre,
-    table,
     table_rows,
     grad_pre,
     grad_moved,
     back_out,
     back_in,
-    child_t,
-    merged_t,
-    parent_t,
     held,
     inbox,
     emb,
@@ -407,19 +448,22 @@
     devices = counts.shape[1]
     cap = slots // devices
     half = slots // 2
-    levels = len(groups[0][2])
+    levels = bias_held.shape[0]
     tiles = width // TILE
     upper = own_bit(hop, core, levels - 2)
     sides = (1 - upper, upper)
     f32, bf16 = jnp.float32, jnp.bfloat16
 
-    def target(rel):
+    def other_hop(flips):
         to_hop = hop
         for bit in range(levels - 1):
-            if (rel >> (bit + 1)) & 1:
+            if (flips >> bit) & 1:
                 to_hop = to_hop + (1 - 2 * own_bit(hop, core, bit)) * (1 << bit)
-        to_core = 1 - core if rel & 1 else core
-        return to_hop, to_core
+        return to_hop
+
+    def targets(first, last):
+        away = [(other_hop(flips), to_core) for to_core in range(2) for flips in range(last - 1, max(first, 1) - 1, -1)]
+        return away + ([(hop, 1 - core)] if first == 0 else [])
 
     def rows_of(device):
         return pl.ds(pl.multiple_of(device * cap, cap), cap)
@@ -431,13 +475,13 @@
     for index, (source, place) in enumerate(
         ((child_in, child), (proj_in, proj), (q_in, q), (parent_in, parent), (w_in, w), (cot_in, cot))
     ):
-        copy = pltpu.make_async_copy(source, place, load_sem.at[index])
+        loads.append(pltpu.make_async_copy(source, place, load_sem.at[index]))
+    for copy in loads[:3]:
         copy.start()
-        loads.append(copy)
 
     barrier = pltpu.get_barrier_semaphore()
-    for rel in range(1, devices):
-        pl.semaphore_signal(barrier, inc=1, device_id=target(rel), device_id_type=MESH)
+    for to in targets(0, devices // 2):
+        pl.semaphore_signal(barrier, inc=1, device_id=to, device_id_type=MESH)
 
     lane = lax.broadcasted_iota(jnp.int32, (128, 128), 1)
     down = lax.broadcasted_iota(jnp.int32, (128, 128), 0)
@@ -466,30 +510,23 @@
                 info[owner_at * cap : (owner_at + 1) * cap, :], axis=0, keepdims=True
             )
 
-    pl.semaphore_wait(barrier, devices - 1)
-
-    for rel in range(devices - 1, 0, -1):
-        to_hop, to_core = target(rel)
-        pltpu.make_async_remote_copy(
-            src_ref=info_out.at[to_hop * 2 + to_core],
-            dst_ref=info_in.at[me],
-            send_sem=info_sem.at[0],
-            recv_sem=info_sem.at[1],
-            device_id=(to_hop, to_core),
-            device_id_type=MESH,
-        ).start()
-    pltpu.make_async_copy(info_out.at[me], info_in.at[me], info_sem.at[1]).start()
+    def send_info():
+        pl.semaphore_wait(barrier, devices - 1)
+
+        for to_hop, to_core in targets(0, devices // 2):
+            pltpu.make_async_remote_copy(
+                src_ref=info_out.at[to_hop * 2 + to_core],
+                dst_ref=info_in.at[me],
+                send_sem=info_sem.at[0],
+                recv_sem=info_sem.at[1],
+                device_id=(to_hop, to_core),
+                device_id_type=MESH,
+            ).start()
+        pltpu.make_async_copy(info_out.at[me], info_in.at[me], info_sem.at[1]).start()
 
     def send_side(source, place_ref, sem, side_index):
-        first = devices // 2 if side_index == 0 else 0
-        rels = sorted(range(first, first + devices // 2), key=lambda rel: (rel & 1, -rel))
-        for rel in rels:
-            if rel == 0:
-                pltpu.make_async_copy(
-                    source.at[rows_of(me)], place_ref.at[rows_of(me)], sem.at[1, side_index]
-                ).start()
-                continue
-            to_hop, to_core = target(rel)
+        quarter = devices // 4
+        for to_hop, to_core in targets(quarter, 2 * quarter) if side_index == 0 else targets(0, quarter):
             pltpu.make_async_remote_copy(
                 src_ref=source.at[rows_of(to_hop * 2 + to_core)],
                 dst_ref=place_ref.at[rows_of(me)],
@@ -498,6 +535,10 @@
                 device_id=(to_hop, to_core),
                 device_id_type=MESH,
             ).start()
+        if side_index == 1:
+            pltpu.make_async_copy(
+                source.at[rows_of(me)], place_ref.at[rows_of(me)], sem.at[1, side_index]
+            ).start()
 
     def wait_side(place_ref, sem, side_index):
         rows = side_rows(sides[side_index])
@@ -522,6 +563,8 @@
 
         if side_index == 0:
             loads[2].wait()
+            for copy in loads[3:]:
+                copy.start()
         weights = spread(weight_col[rows, :], TILE)
 
         @pl.loop(0, tiles)
@@ -532,6 +575,8 @@
             message[rows, columns(tile)] = (weights * act).astype(bf16)
             scaled_slope[rows, columns(tile)] = weights * (gate + act * (1.0 - gate))
 
+        if side_index == 0:
+            send_info()
         send_side(message, arrived, msg_sem, side_index)
 
     loads[3].wait()
@@ -539,12 +584,7 @@
 
     @pl.loop(0, tiles)
     def _(tile):
-        @pl.loop(0, parents // 512)
-        def _(block):
-            pre[columns(block, 512), columns(tile)] = (
-                mm(parent[columns(block, 512), :], w[pl.ds(0, width), columns(tile)])
-                + w_bias[:, columns(tile)]
-            )
+        pre[:, columns(tile)] = mm(parent[...], w[pl.ds(0, width), columns(tile)]) + w_bias[:, columns(tile)]
 
     info_all = pltpu.make_async_copy(info_in, info_in, info_sem.at[1])
     info_all.wait()
@@ -584,22 +624,8 @@
             jnp.sum(slot_shrink[at, :], axis=1, keepdims=True), (128, 128)
         )
 
-    def transpose_into(place_ref, source, blocks):
-        for block in range(blocks):
-
-            @pl.loop(0, source.shape[1] // TILE)
-            def _(tile):
-                part = source[block * TILE : (block + 1) * TILE, columns(tile)]
-                place_ref[block, columns(tile), :] = part.T
-
-    transpose_into(table, table_rows, slots // TILE)
-    transpose_into(child_t, child, slots // TILE)
-    transpose_into(merged_t, merged, slots // TILE)
-    transpose_into(parent_t, parent, parents // TILE)
-
     def add_messages(side_index):
-        side = sides[side_index]
-        rows = side_rows(side)
+        rows = side_rows(sides[side_index])
 
         @pl.loop(0, tiles)
         def _(tile):
@@ -607,12 +633,9 @@
 
         @pl.loop(0, tiles)
         def _(tile):
-            @pl.loop(0, parents // 512)
-            def _(block):
-                at = columns(block, 512)
-                pre[at, columns(tile)] = pre[at, columns(tile)] + spread(shrink[at, :], TILE) * mm(
-                    table[side, at, :], moved[rows, columns(tile)]
-                )
+            pre[:, columns(tile)] = pre[:, columns(tile)] + spread(shrink[...], TILE) * contract_rows(
+                table_rows[rows, :], moved[rows, columns(tile)]
+            )
 
     wait_side(arrived, msg_sem, 1)
     add_messages(1)
@@ -659,52 +682,30 @@
 
     @pl.loop(0, tiles)
     def _(tile):
-        @pl.loop(0, tiles)
-        def _(block):
-            total_part = jnp.zeros((TILE, TILE), f32)
-            for part in range(parents // TILE):
-                total_part = total_part + mm(
-                    parent_t[part, columns(block), :],
-                    grad_pre[part * TILE : (part + 1) * TILE, columns(tile)],
-                )
-            held[columns(block), columns(tile)] = total_part.astype(bf16)
+        held[pl.ds(0, width), columns(tile)] = contract_rows(parent[...], grad_pre[:, columns(tile)]).astype(bf16)
 
     for group in w_groups[: len(w_groups) // 2]:
         sums.halve(group, 0)
-    transpose_into(table, arrived, slots // TILE)
 
     @pl.loop(0, tiles)
     def _(tile):
-        @pl.loop(0, tiles)
-        def _(block):
-            total_part = jnp.zeros((TILE, TILE), f32)
-            for part in range(slots // TILE):
-                total_part = total_part + mm(
-                    table[part, columns(block), :],
-                    grad_moved[part * TILE : (part + 1) * TILE, columns(tile)],
-                )
-            at = pl.ds(pl.multiple_of(width + block * TILE, TILE), TILE)
-            held[at, columns(tile)] = total_part.astype(bf16)
+        held[pl.ds(width, width), columns(tile)] = contract_rows(
+            arrived[...], grad_moved[:, columns(tile)]
+        ).astype(bf16)
 
     for group in w_groups[len(w_groups) // 2 :]:
         sums.halve(group, 0)
     bias_held[0] = jnp.zeros(bias_held.shape[1:], f32)
     bias_held[0, 0:1, :] = mm(jnp.ones((16, parents), bf16), grad_pre[...])[0:1, :]
 
-    for group in w_groups:
-        sums.fold(group, 0)
-
-    @pl.loop(0, tiles)
-    def _(tile):
-        @pl.loop(0, parents // 512)
-        def _(block):
-            parent[columns(block, 512), columns(tile)] = times_transpose(
-                grad_pre[columns(block, 512), :], w[columns(tile), :]
-            ).astype(bf16)
-
-    stores.append(pltpu.make_async_copy(parent, parent_out, store_sem.at[1]))
-    stores[1].start()
-    wait_sent(message, msg_sem)
+    def parent_gradient():
+        @pl.loop(0, tiles)
+        def _(tile):
+            parent[:, columns(tile)] = times_transpose(grad_pre[...], w[columns(tile), :]).astype(bf16)
+
+        stores.append(pltpu.make_async_copy(parent, parent_out, store_sem.at[1]))
+        stores[1].start()
+        wait_sent(message, msg_sem)
 
     def child_front(side_index):
         rows = side_rows(sides[side_index])
@@ -715,21 +716,16 @@
                 scaled_slope[rows, columns(tile)] * back_in[rows, columns(tile)].astype(f32)
             ).astype(bf16)
 
-    def weight_sums(side_index, turned, grads, partial, base):
-        side = sides[side_index]
-        rows = side_rows(side)
+    def weight_sums(side_index, left, grads, partial, base):
+        rows = side_rows(sides[side_index])
 
         @pl.loop(0, tiles)
         def _(tile):
-            @pl.loop(0, width // 512)
-            def _(block):
-                at = columns(block, 512)
-                value = mm(turned[side, at, :], grads[rows, columns(tile)])
-                if side_index == 1:
-                    partial[at, columns(tile)] = value
-                else:
-                    place_at = pl.ds(pl.multiple_of(base + block * 512, 512), 512)
-                    held[place_at, columns(tile)] = (value + partial[at, columns(tile)]).astype(bf16)
+            value = contract_rows(left[rows, :], grads[rows, columns(tile)])
+            if side_index == 1:
+                partial[:, columns(tile)] = value
+            else:
+                held[pl.ds(base, width), columns(tile)] = (value + partial[:, columns(tile)]).astype(bf16)
 
     def child_middle(side_index):
         rows = side_rows(sides[side_index])
@@ -749,27 +745,6 @@
             value = times_transpose(moved[rows, :], proj[columns(tile), :])
             message[rows, columns(tile)] = (scaled_slope[rows, columns(tile)] + value).astype(bf16)
 
-    wait_side(back_in, back_sem, 1)
-    child_front(1)
-    weight_sums(1, merged_t, grad_moved, pre, 2 * width)
-    child_middle(1)
-    weight_sums(1, child_t, moved, cot, 3 * width)
-    child_end(1)
-
-    for group in w_groups:
-        sums.fold(group, 1)
-
-    wait_side(back_in, back_sem, 0)
-    child_front(0)
-    weight_sums(0, merged_t, grad_moved, pre, 2 * width)
-    for group in q_groups:
-        sums.halve(group, 0)
-    child_middle(0)
-    weight_sums(0, child_t, moved, cot, 3 * width)
-    for group in p_groups:
-        sums.halve(group, 0)
-
-    bias_held[0, 1:2, :] = mm(jnp.ones((16, slots), bf16), grad_moved[...])[0:1, :]
     bias_copies = []
 
     def send_bias(level):
@@ -778,7 +753,7 @@
             dst_ref=bias_in.at[level],
             send_sem=bias_sem.at[0, level],
             recv_sem=bias_sem.at[1, level],
-            device_id=partner(hop, core, groups[0][2][level]),
+            device_id=partner(hop, core, level - 1),
             device_id_type=MESH,
         )
         copy.start()
@@ -793,20 +768,49 @@
         else:
             bias_out[...] = both
 
-    send_bias(0)
-    child_end(0)
-    stores.append(pltpu.make_async_copy(message, child_out, store_sem.at[2]))
-    stores[2].start()
-
-    late = q_groups + p_groups
-    plan = [("late", 0), ("w", 2), ("late", 1), ("w", 3), ("late", 2), ("w", 4), ("late", 3), ("w_up", 4)]
-    plan += [("late", 4), ("w_up", 3), ("late_up", 4), ("w_up", 2), ("late_up", 3), ("w_up", 1)]
-    plan += [("late_up", 2), ("w_up", 0), ("late_up", 1), ("late_up", 0)]
-    for what, level in plan:
-        for group in w_groups if what[0] == "w" else late:
-            (sums.gather if what.endswith("up") else sums.fold)(group, level)
-        if what == "late":
-            fold_bias(level)
+    def near_children():
+        child_front(1)
+        weight_sums(1, merged, grad_moved, pre, 2 * width)
+        child_middle(1)
+        weight_sums(1, child, moved, cot, 3 * width)
+        child_end(1)
+
+    def far_q():
+        child_front(0)
+        weight_sums(0, merged, grad_moved, pre, 2 * width)
+
+    def far_p():
+        child_middle(0)
+        weight_sums(0, child, moved, cot, 3 * width)
+
+    def far_end():
+        bias_held[0, 1:2, :] = mm(jnp.ones((16, slots), bf16), grad_moved[...])[0:1, :]
+        send_bias(0)
+        child_end(0)
+        stores.append(pltpu.make_async_copy(message, child_out, store_sem.at[2]))
+        stores[2].start()
+
+    main = [
+        parent_gradient,
+        lambda: wait_side(back_in, back_sem, 1),
+        near_children,
+        lambda: wait_side(back_in, back_sem, 0),
+        far_q,
+        lambda: [sums.halve(group, 0) for group in q_groups],
+        far_p,
+        lambda: [sums.halve(group, 0) for group in p_groups],
+        far_end,
+    ] + [functools.partial(fold_bias, level) for level in range(levels)]
+    done = [0] * (len(groups) + 1)
+    for turn in SCHEDULE:
+        at = done[turn]
+        done[turn] += 1
+        if turn == 0:
+            main[at]()
+        elif at < sums.levels:
+            sums.fold(turn - 1, at)
+        else:
+            sums.gather(turn - 1, 2 * sums.levels - 1 - at)
 
     sums.finish()
     for copy in bias_copies:
@@ -818,12 +822,124 @@
         copy.wait()
 
 
+ORDERS = ["cxyim", "cyxim", "cxyim", "cyxim", "cxyim", "cyxim", "cxyim", "cyxim"]
+SCHEDULE = [
+    3, 0, 4, 1, 3, 0, 0, 4, 1, 2, 0, 0, 0, 0, 0, 4, 1, 2, 1, 7, 3, 8, 4, 1, 2, 3, 4, 2, 7, 8, 3, 5, 6, 3, 7, 4,
+    8, 2, 1, 7, 5, 6, 2, 3, 4, 1, 7, 8, 2, 6, 5, 4, 8, 7, 0, 6, 1, 7, 2, 0, 5, 8, 8, 6, 0, 5, 6, 5, 1, 0, 4, 7,
+    6, 5, 0, 8, 5, 6, 3, 0, 7, 2, 5, 8, 2, 6, 5, 3, 1, 8, 6, 4, 7, 3,
+]
+
+
 def sum_groups(width):
-    x, y, z0, z1 = range(4)
-    orders = [[x, y, z0, z1], [y, x, z0, z1], [x, z0, y, z1], [y, z0, x, z1]]
-    orders += [[x, y, z0, z1], [y, x, z0, z1], [z0, x, y, z1], [z0, y, x, z1]]
-    rows = 4 * width // len(orders)
-    return [(index * rows, rows, [CORE] + order) for index, order in enumerate(orders)]
+    rows = 4 * width // len(ORDERS)
+    return [(index * rows, rows, order) for index, order in enumerate(ORDERS)]
+
+
+def inbox_rows(groups):
+    total = 0
+    for _, size, order in groups:
+        for kind in order:
+            size = size if kind == "i" else size // 2
+            total += size
+    return total
+
+
+def widen_kernel(
+    emb,
+    child,
+    parent,
+    total,
+    biases,
+    emb_out,
+    child_out,
+    parent_out,
+    proj_out,
+    q_out,
+    q_bias_out,
+    w_out,
+    w_bias_out,
+    narrow,
+    wide,
+    through,
+    read_sem,
+    write_sem,
+    child_sem,
+):
+    slots, rows, width = narrow.shape
+    through_in = pltpu.make_async_copy(child, through, child_sem.at[0])
+    through_out = pltpu.make_async_copy(through, child_out, child_sem.at[1])
+    pieces = []
+    base = 0
+    for place in (w_out, q_out, proj_out):
+        for first in range(0, place.shape[0], rows):
+            pieces.append((total, base + first, place, first))
+        base += place.shape[0]
+    for source, place in ((parent, parent_out), (emb, emb_out)):
+        for first in range(0, place.shape[0], rows):
+            pieces.append((source, first, place, first))
+
+    def read(index):
+        source, first, _, _ = pieces[index]
+        slot = index % slots
+        return pltpu.make_async_copy(source.at[pl.ds(first, rows)], narrow.at[slot], read_sem.at[slot])
+
+    def write(index):
+        _, _, place, first = pieces[index]
+        slot = index % slots
+        return pltpu.make_async_copy(wide.at[slot], place.at[pl.ds(first, rows)], write_sem.at[slot])
+
+    for index in range(slots):
+        read(index).start()
+    through_in.start()
+    w_bias_out[...] = biases[0, :]
+    q_bias_out[...] = biases[1, :]
+    for index in range(len(pieces)):
+        read(index).wait()
+        if index >= slots:
+            write(index - slots).wait()
+        wide[index % slots] = narrow[index % slots].astype(jnp.float32)
+        write(index).start()
+        if index + slots < len(pieces):
+            read(index + slots).start()
+        if index == slots:
+            through_in.wait()
+            through_out.start()
+    for index in range(len(pieces) - slots, len(pieces)):
+        write(index).wait()
+    through_out.wait()
+
+
+def widen(emb, child, parent, total, biases):
+    width = emb.shape[1]
+    slots, rows = 4, 512
+    shape, f32 = jax.ShapeDtypeStruct, jnp.float32
+    hbm = pl.BlockSpec(memory_space=pl.ANY)
+    vmem = pl.BlockSpec(memory_space=pltpu.VMEM)
+    return pl.pallas_call(
+        widen_kernel,
+        name="widen",
+        out_shape=(
+            shape(emb.shape, f32),
+            shape(child.shape, child.dtype),
+            shape(parent.shape, f32),
+            shape((width, width), f32),
+            shape((width, width), f32),
+            shape((width,), f32),
+            shape((2 * width, width), f32),
+            shape((width,), f32),
+        ),
+        in_specs=[hbm, hbm, hbm, hbm, vmem],
+        out_specs=(hbm, hbm, hbm, hbm, hbm, vmem, hbm, vmem),
+        scratch_shapes=[
+            pltpu.VMEM((slots, rows, width), child.dtype),
+            pltpu.VMEM((slots, rows, width), f32),
+            pltpu.VMEM(child.shape, child.dtype),
+            pltpu.SemaphoreType.DMA((slots,)),
+            pltpu.SemaphoreType.DMA((slots,)),
+            pltpu.SemaphoreType.DMA((2,)),
+        ],
+        compiler_params=pltpu.CompilerParams(vmem_limit_bytes=62 << 20),
+    )(emb, child, parent, total, biases)
 
 
 def fused_body(
@@ -844,9 +960,8 @@
     parents = parent_feats.shape[0]
     devices = send_counts.shape[1]
     groups = sum_groups(width)
-    levels = len(groups[0][2])
+    levels = devices.bit_length() - 1
     f32, bf16 = jnp.float32, jnp.bfloat16
-    half = slots // 2
     vmem = pl.BlockSpec(memory_space=pltpu.VMEM)
     hbm = pl.BlockSpec(memory_space=pl.ANY)
     dma = pltpu.SemaphoreType.DMA
@@ -876,17 +991,13 @@
             pltpu.VMEM((slots, width), bf16),
             pltpu.VMEM((slots, width), bf16),
             pltpu.VMEM((parents, width), f32),
-            pltpu.VMEM((2, parents, half), bf16),
             pltpu.VMEM((slots, parents), bf16),
             pltpu.VMEM((parents, width), bf16),
             pltpu.VMEM((slots, width), bf16),
             pltpu.VMEM((slots, width), bf16),
             pltpu.VMEM((slots, width), bf16),
-            pltpu.VMEM((2, width, half), bf16),
-            pltpu.VMEM((2, width, half), bf16),
-            pltpu.VMEM((parents // TILE, width, TILE), bf16),
             pltpu.VMEM((4 * width, width), bf16),
-            pltpu.VMEM((4 * width, width), bf16),
+            pltpu.VMEM((inbox_rows(groups), width), bf16),
             pltpu.VMEM((parents, width), bf16),
             pltpu.VMEM((slots, 128), f32),
             pltpu.VMEM((slots, 128), f32),
@@ -905,7 +1016,7 @@
             dma((2, 2)),
             dma((2, levels)),
         ]
-        + [dma((len(groups), levels))] * 4
+        + [dma((len(groups), len(groups[0][2])))] * 4
         + [dma((len(groups),))],
         compiler_params=pltpu.CompilerParams(
             collective_id=1, has_side_effects=True, vmem_limit_bytes=62 << 20
@@ -927,16 +1038,7 @@
         w_bias.reshape(1, -1),
         emb_cotangent,
     )
-    return (
-        emb.astype(f32),
-        grad_child,
-        grad_parent.astype(f32),
-        total[3 * width :].astype(f32),
-        total[2 * width : 3 * width].astype(f32),
-        biases[1],
-        total[: 2 * width].astype(f32),
-        biases[0],
-    )
+    return widen(emb, grad_child, grad_parent, total, biases)
 
 
 def solution(mesh):

time: 181 us -> 152 us (0.84); the launches traced: 179 us -> 152 us
  other arithmetic: 16.2 us -> 0 us
  Pallas kernels: 159 us -> 151 us
  local copies, waits for them, and re-layouts: 2.51 us -> 0 us
    pallas_call x1, Pallas kernels: 159 us -> 136 us  [fused_body(): pl.pallas_call(functools.partial(layer_kernel, groups), name='layer', out...]
    convert_element_type x4 -> x0, other arithmetic: 16.2 us -> none  [the longest x1 6.83 us: fused_body(): total[2 * width:3 * width].astype(f32)]
    pallas_call x0 -> x1, Pallas kernels: none -> 14.3 us  [widen(): pl.pallas_call(widen_kernel, name='widen', out_shape=(shape(emb.shape, f3...]
where the time goes in v3:
time: 152 us
  Pallas kernels  151 us (99%)
    pallas_call x1, Pallas kernels, fused_body(): pl.pallas_call(functools.partial(layer_kernel, groups), name='layer', out...  136 us
    pallas_call x1, Pallas kernels, widen(): pl.pallas_call(widen_kernel, name='widen', out_shape=(shape(emb.shape, f3...  14.3 us

profile of v3, /device:TPU:0, one launch (start us, length us, event | category | flops | bytes accessed | tf_op | source)
XLA Modules:
  0.0 151.6 jit_solution(15723535205803781592)
XLA Ops:
  0.6 136.5 %layer.1 = (bf16[1024,1024]{1,0:T(8,128)(2,1)}, bf16[512,1024]{1,0:T(8,128)(2,1)}, bf16[1024,1024]{1,0:T(8,128)(2,1)}, bf16[4096,1024]{1,0:T(8,128)(2,1)}, f32[8,1024]{1,0:T(8,128)}) custom-call(bf16[512,1024]{1,0:T(8,128)(2,1)} %child_in.1, f32[4,128]{1,0:T(4,128)} %bitcast.7, s32[4,128]{1,0:T(4,128)} %bitcast.8, s32[4,128]{1,0:T(4,128)} %bitcast.9, ...), custom_call_target="tpu_custom_call" | custom-call | flops 19327352832 | bytes 41943040 | tf_op jit(solution)/shard_map/layer/pallas_call | solution.py:969
  137.1 14.3 %widen.1 = (f32[1024,1024]{1,0:T(8,128)}, bf16[512,1024]{1,0:T(8,128)(2,1)}, f32[1024,1024]{1,0:T(8,128)}, f32[1024,1024]{1,0:T(8,128)}, f32[1024,1024]{1,0:T(8,...) custom-call(bf16[1024,1024]{1,0:T(8,128)(2,1)} %get-tuple-element.13.emb, ...), custom_call_target="tpu_custom_call" | custom-call | tf_op jit(solution)/shard_map/widen/pallas_call | solution.py:918

commit v4 on v3

--- a/solution.py
+++ b/solution.py
@@ -695,7 +695,6 @@
 
     for group in w_groups[len(w_groups) // 2 :]:
         sums.halve(group, 0)
-    bias_held[0] = jnp.zeros(bias_held.shape[1:], f32)
     bias_held[0, 0:1, :] = mm(jnp.ones((16, parents), bf16), grad_pre[...])[0:1, :]
 
     def parent_gradient():
@@ -783,9 +782,13 @@
         child_middle(0)
         weight_sums(0, child, moved, cot, 3 * width)
 
-    def far_end():
+    def send_q():
+        for group in q_groups:
+            sums.halve(group, 0)
         bias_held[0, 1:2, :] = mm(jnp.ones((16, slots), bf16), grad_moved[...])[0:1, :]
         send_bias(0)
+
+    def far_end():
         child_end(0)
         stores.append(pltpu.make_async_copy(message, child_out, store_sem.at[2]))
         stores[2].start()
@@ -796,11 +799,11 @@
         near_children,
         lambda: wait_side(back_in, back_sem, 0),
         far_q,
-        lambda: [sums.halve(group, 0) for group in q_groups],
+        send_q,
         far_p,
         lambda: [sums.halve(group, 0) for group in p_groups],
         far_end,
-    ] + [functools.partial(fold_bias, level) for level in range(levels)]
+    ]
     done = [0] * (len(groups) + 1)
     for turn in SCHEDULE:
         at = done[turn]
@@ -809,6 +812,8 @@
             main[at]()
         elif at < sums.levels:
             sums.fold(turn - 1, at)
+            if turn - 1 == q_groups[0]:
+                fold_bias(at)
         else:
             sums.gather(turn - 1, 2 * sums.levels - 1 - at)
 
@@ -822,17 +827,21 @@
         copy.wait()
 
 
-ORDERS = ["cxyim", "cyxim", "cxyim", "cyxim", "cxyim", "cyxim", "cxyim", "cyxim"]
+GROUPS = [("cxyim", 2), ("cyxim", 2), ("cxyim", 2), ("cyxim", 2), ("cxyim", 4), ("cyxim", 4), ("cxyim", 4), ("cyxim", 4), ("cxyim", 4), ("cyxim", 4), ("cxyim", 4), ("cyxim", 4)]
 SCHEDULE = [
-    3, 0, 4, 1, 3, 0, 0, 4, 1, 2, 0, 0, 0, 0, 0, 4, 1, 2, 1, 7, 3, 8, 4, 1, 2, 3, 4, 2, 7, 8, 3, 5, 6, 3, 7, 4,
-    8, 2, 1, 7, 5, 6, 2, 3, 4, 1, 7, 8, 2, 6, 5, 4, 8, 7, 0, 6, 1, 7, 2, 0, 5, 8, 8, 6, 0, 5, 6, 5, 1, 0, 4, 7,
-    6, 5, 0, 8, 5, 6, 3, 0, 7, 2, 5, 8, 2, 6, 5, 3, 1, 8, 6, 4, 7, 3,
+    3, 4, 0, 1, 2, 0, 0, 3, 4, 0, 0, 0, 1, 2, 3, 4, 0, 5, 6, 0, 11, 12, 9, 10, 3, 4, 0, 1, 2, 7, 8, 3, 4, 5, 6, 1,
+    2, 11, 12, 3, 4, 9, 10, 5, 6, 1, 2, 7, 8, 11, 12, 3, 4, 9, 10, 7, 8, 5, 6, 1, 2, 3, 4, 11, 12, 1, 2, 9, 10, 5, 6, 7,
+    8, 5, 6, 11, 12, 1, 2, 5, 6, 9, 10, 11, 12, 7, 8, 9, 10, 11, 12, 3, 4, 9, 10, 7, 8, 7, 8, 5, 6, 11, 12, 1, 2, 9, 10, 5,
+    6, 7, 8, 3, 4, 11, 12, 9, 10, 7, 8, 5, 6, 1, 2, 11, 12, 9, 10, 7, 8,
 ]
 
 
 def sum_groups(width):
-    rows = 4 * width // len(ORDERS)
-    return [(index * rows, rows, order) for index, order in enumerate(ORDERS)]
+    groups, first = [], 0
+    for order, share in GROUPS:
+        groups.append((first, width // share, order))
+        first += width // share
+    return groups
 
 
 def inbox_rows(groups):
@@ -974,7 +983,7 @@
             shape((slots, width), bf16),
             shape((parents, width), bf16),
             shape((4 * width, width), bf16),
-            shape((8, width), f32),
+            shape((2, width), f32),
         ),
         in_specs=[hbm, vmem, vmem, vmem, vmem, hbm, hbm, hbm, vmem, hbm, vmem, hbm],
         out_specs=(hbm, hbm, hbm, hbm, vmem),
@@ -1007,8 +1016,8 @@
             pltpu.VMEM((slots, 128), f32),
             pltpu.VMEM((devices, 1, 128), f32),
             pltpu.VMEM((devices, 1, 128), f32),
-            pltpu.VMEM((levels, 8, width), f32),
-            pltpu.VMEM((levels, 8, width), f32),
+            pltpu.VMEM((levels, 2, width), f32),
+            pltpu.VMEM((levels, 2, width), f32),
             dma((6,)),
             dma((3,)),
             dma((2,)),

time: 152 us -> 146 us (0.961)
  Pallas kernels: 151 us -> 145 us
    pallas_call x1, Pallas kernels: 136 us -> 131 us  [fused_body(): pl.pallas_call(functools.partial(layer_kernel, groups), name='layer', out...]
where the time goes in v4:
time: 146 us
  Pallas kernels  145 us (99%)
    pallas_call x1, Pallas kernels, fused_body(): pl.pallas_call(functools.partial(layer_kernel, groups), name='layer', out...  131 us
    pallas_call x1, Pallas kernels, widen(): pl.pallas_call(widen_kernel, name='widen', out_shape=(shape(emb.shape, f3...  14.3 us

profile of v4, /device:TPU:0, one launch (start us, length us, event | category | flops | bytes accessed | tf_op | source)
XLA Modules:
  0.0 146.2 jit_solution(11066663601627656696)
XLA Ops:
  0.6 131.1 %layer.1 = (bf16[1024,1024]{1,0:T(8,128)(2,1)}, bf16[512,1024]{1,0:T(8,128)(2,1)}, bf16[1024,1024]{1,0:T(8,128)(2,1)}, bf16[4096,1024]{1,0:T(8,128)(2,1)}, f32[2,1024]{1,0:T(2,128)}) custom-call(bf16[512,1024]{1,0:T(8,128)(2,1)} %child_in.1, f32[4,128]{1,0:T(4,128)} %bitcast.7, s32[4,128]{1,0:T(4,128)} %bitcast.8, s32[4,128]{1,0:T(4,128)} %bitcast.9, ...), custom_call_target="tpu_custom_call" | custom-call | flops 19327352832 | bytes 41943040 | tf_op jit(solution)/shard_map/layer/pallas_call | solution.py:978
  131.7 14.3 %widen.1 = (f32[1024,1024]{1,0:T(8,128)}, bf16[512,1024]{1,0:T(8,128)(2,1)}, f32[1024,1024]{1,0:T(8,128)}, f32[1024,1024]{1,0:T(8,128)}, f32[1024,1024]{1,0:T(8,...) custom-call(bf16[1024,1024]{1,0:T(8,128)(2,1)} %get-tuple-element.13.emb, ...), custom_call_target="tpu_custom_call" | custom-call | tf_op jit(solution)/shard_map/widen/pallas_call | solution.py:927

commit v5 on v4

--- a/solution.py
+++ b/solution.py
@@ -394,20 +394,18 @@
     w_in,
     w_bias,
     cot_in,
-    emb_out,
-    child_out,
-    parent_out,
+    emb,
+    message,
+    parent,
     total,
     bias_out,
     child,
     proj,
     q,
     w,
-    parent,
     cot,
     merged,
     scaled_slope,
-    message,
     arrived,
     moved,
     pre,
@@ -418,7 +416,6 @@
     back_in,
     held,
     inbox,
-    emb,
     weight_col,
     board_col,
     shrink,
@@ -430,7 +427,6 @@
     bias_held,
     bias_in,
     load_sem,
-    store_sem,
     info_sem,
     msg_sem,
     back_sem,
@@ -655,9 +651,6 @@
         emb[at, :] = (act * inv).astype(bf16)
         grad_pre[at, :] = ((turn * inv - act * share) * (gate + act * (1.0 - gate))).astype(bf16)
 
-    stores = [pltpu.make_async_copy(emb, emb_out, store_sem.at[0])]
-    stores[0].start()
-
     for side_index, side in enumerate(sides):
         rows = side_rows(side)
         shrinks = spread(slot_shrink[rows, :], TILE)
@@ -702,8 +695,6 @@
         def _(tile):
             parent[:, columns(tile)] = times_transpose(grad_pre[...], w[columns(tile), :]).astype(bf16)
 
-        stores.append(pltpu.make_async_copy(parent, parent_out, store_sem.at[1]))
-        stores[1].start()
         wait_sent(message, msg_sem)
 
     def child_front(side_index):
@@ -790,8 +781,6 @@
 
     def far_end():
         child_end(0)
-        stores.append(pltpu.make_async_copy(message, child_out, store_sem.at[2]))
-        stores[2].start()
 
     main = [
         parent_gradient,
@@ -823,8 +812,6 @@
     wait_sent(back_out, back_sem)
     sent = info_out.at[pl.ds(0, devices - 1)]
     pltpu.make_async_copy(sent, sent, info_sem.at[0]).wait()
-    for copy in stores:
-        copy.wait()
 
 
 GROUPS = [("cxyim", 2), ("cyxim", 2), ("cxyim", 2), ("cyxim", 2), ("cxyim", 4), ("cyxim", 4), ("cxyim", 4), ("cyxim", 4), ("cxyim", 4), ("cyxim", 4), ("cxyim", 4), ("cyxim", 4)]
@@ -869,23 +856,22 @@
     w_bias_out,
     narrow,
     wide,
-    through,
     read_sem,
     write_sem,
     child_sem,
 ):
     slots, rows, width = narrow.shape
-    through_in = pltpu.make_async_copy(child, through, child_sem.at[0])
-    through_out = pltpu.make_async_copy(through, child_out, child_sem.at[1])
+    through = pltpu.make_async_copy(child, child_out, child_sem)
     pieces = []
+    for source, place in ((parent, parent_out), (emb, emb_out)):
+        for first in range(0, place.shape[0], rows):
+            pieces.append((source, first, place, first))
     base = 0
     for place in (w_out, q_out, proj_out):
         for first in range(0, place.shape[0], rows):
             pieces.append((total, base + first, place, first))
         base += place.shape[0]
-    for source, place in ((parent, parent_out), (emb, emb_out)):
-        for first in range(0, place.shape[0], rows):
-            pieces.append((source, first, place, first))
+    near = [True for source, _, _, _ in pieces]
 
     def read(index):
         source, first, _, _ = pieces[index]
@@ -897,25 +883,28 @@
         slot = index % slots
         return pltpu.make_async_copy(wide.at[slot], place.at[pl.ds(first, rows)], write_sem.at[slot])
 
-    for index in range(slots):
+    far = [index for index in range(len(pieces)) if not near[index]]
+    for index in far[:slots]:
         read(index).start()
-    through_in.start()
+    for index in range(len(pieces)):
+        source, first, _, _ = pieces[index]
+        if index >= slots:
+            write(index - slots).wait()
+        if near[index]:
+            value = source[first : first + rows, :]
+        else:
+            read(index).wait()
+            value = narrow[index % slots]
+        wide[index % slots] = value.astype(jnp.float32)
+        write(index).start()
+        if not near[index] and index + slots < len(pieces):
+            read(index + slots).start()
+    through.start()
     w_bias_out[...] = biases[0, :]
     q_bias_out[...] = biases[1, :]
-    for index in range(len(pieces)):
-        read(index).wait()
-        if index >= slots:
-            write(index - slots).wait()
-        wide[index % slots] = narrow[index % slots].astype(jnp.float32)
-        write(index).start()
-        if index + slots < len(pieces):
-            read(index + slots).start()
-        if index == slots:
-            through_in.wait()
-            through_out.start()
     for index in range(len(pieces) - slots, len(pieces)):
         write(index).wait()
-    through_out.wait()
+    through.wait()
 
 
 def widen(emb, child, parent, total, biases):
@@ -937,17 +926,16 @@
             shape((2 * width, width), f32),
             shape((width,), f32),
         ),
-        in_specs=[hbm, hbm, hbm, hbm, vmem],
+        in_specs=[vmem, vmem, vmem, vmem, vmem],
         out_specs=(hbm, hbm, hbm, hbm, hbm, vmem, hbm, vmem),
         scratch_shapes=[
             pltpu.VMEM((slots, rows, width), child.dtype),
             pltpu.VMEM((slots, rows, width), f32),
-            pltpu.VMEM(child.shape, child.dtype),
             pltpu.SemaphoreType.DMA((slots,)),
             pltpu.SemaphoreType.DMA((slots,)),
-            pltpu.SemaphoreType.DMA((2,)),
+            pltpu.SemaphoreType.DMA,
         ],
-        compiler_params=pltpu.CompilerParams(vmem_limit_bytes=62 << 20),
+        compiler_params=pltpu.CompilerParams(vmem_limit_bytes=36 << 20),
     )(emb, child, parent, total, biases)
 
 
@@ -979,24 +967,22 @@
         functools.partial(layer_kernel, groups),
         name="layer",
         out_shape=(
-            shape((parents, width), bf16),
-            shape((slots, width), bf16),
-            shape((parents, width), bf16),
-            shape((4 * width, width), bf16),
+            pltpu.VMEM((parents, width), bf16),
+            pltpu.VMEM((slots, width), bf16),
+            pltpu.VMEM((parents, width), bf16),
+            pltpu.VMEM((4 * width, width), bf16),
             shape((2, width), f32),
         ),
         in_specs=[hbm, vmem, vmem, vmem, vmem, hbm, hbm, hbm, vmem, hbm, vmem, hbm],
-        out_specs=(hbm, hbm, hbm, hbm, vmem),
+        out_specs=(vmem, vmem, vmem, vmem, vmem),
         scratch_shapes=[
             pltpu.VMEM((slots, width), bf16),
             pltpu.VMEM((width, width), bf16),
             pltpu.VMEM((width, width), bf16),
             pltpu.VMEM((2 * width, width), bf16),
-            pltpu.VMEM((parents, width), bf16),
             pltpu.VMEM((parents, width), f32),
             pltpu.VMEM((slots, width), bf16),
             pltpu.VMEM((slots, width), f32),
-            pltpu.VMEM((slots, width), bf16),
             pltpu.VMEM((slots, width), bf16),
             pltpu.VMEM((slots, width), bf16),
             pltpu.VMEM((parents, width), f32),
@@ -1007,7 +993,6 @@
             pltpu.VMEM((slots, width), bf16),
             pltpu.VMEM((4 * width, width), bf16),
             pltpu.VMEM((inbox_rows(groups), width), bf16),
-            pltpu.VMEM((parents, width), bf16),
             pltpu.VMEM((slots, 128), f32),
             pltpu.VMEM((slots, 128), f32),
             pltpu.VMEM((parents, 128), f32),
@@ -1019,7 +1004,6 @@
             pltpu.VMEM((levels, 2, width), f32),
             pltpu.VMEM((levels, 2, width), f32),
             dma((6,)),
-            dma((3,)),
             dma((2,)),
             dma((2, 2)),
             dma((2, 2)),
@@ -1028,7 +1012,7 @@
         + [dma((len(groups), len(groups[0][2])))] * 4
         + [dma((len(groups),))],
         compiler_params=pltpu.CompilerParams(
-            collective_id=1, has_side_effects=True, vmem_limit_bytes=62 << 20
+            collective_id=1, has_side_effects=True, vmem_limit_bytes=50 << 20
         ),
         cost_estimate=pl.CostEstimate(
             flops=36 * slots * width * width, bytes_accessed=40 << 20, transcendentals=3 * parents * width

time: 146 us -> 141 us (0.966)
  Pallas kernels: 145 us -> 139 us
    pallas_call x1, Pallas kernels: 14.3 us -> 9.5 us  [widen(): pl.pallas_call(widen_kernel, name='widen', out_shape=(shape(emb.shape, f3...]
    pallas_call x1, Pallas kernels: 131 us -> 129 us  [fused_body(): pl.pallas_call(functools.partial(layer_kernel, groups), name='layer', out...]
where the time goes in v5:
time: 141 us; the launch traced here: 140 us
  Pallas kernels  139 us (99%)
    pallas_call x1, Pallas kernels, fused_body(): pl.pallas_call(functools.partial(layer_kernel, groups), name='layer', out...  129 us
    pallas_call x1, Pallas kernels, widen(): pl.pallas_call(widen_kernel, name='widen', out_shape=(shape(emb.shape, f3...  9.5 us

profile of v5, /device:TPU:0, one launch (start us, length us, event | category | flops | bytes accessed | tf_op | source)
XLA Modules:
  0.0 140.3 jit_solution(16278614059411430692)
XLA Ops:
  0.6 129.3 %layer.1 = (bf16[1024,1024]{1,0:T(8,128)(2,1)S(1)}, bf16[512,1024]{1,0:T(8,128)(2,1)S(1)}, bf16[1024,1024]{1,0:T(8,128)(2,1)S(1)}, bf16[4096,1024]{1,0:T(8,128)(2,1)S(1)}, f32[2,1024]{1,0:T(2,128)}) custom-call(bf16[512,1024]{1,0:T(8,128)(2,1)} %child_in.1, f32[4,128]{1,0:T(4,128)} %bitcast.7, s32[4,128]{1,0:T(4,128)} %bitcast.8, s32[4,128]{1,0:T(4,128)} %bitcast.9, ...), custom_call_target="tpu_custom_call" | custom-call | flops 19327352832 | bytes 41943040 | tf_op jit(solution)/shard_map/layer/pallas_call | solution.py:966
  130.0 0.0 copy-start
  130.0 0.7 copy-done
  130.7 9.5 %widen.1 = (f32[1024,1024]{1,0:T(8,128)}, bf16[512,1024]{1,0:T(8,128)(2,1)}, f32[1024,1024]{1,0:T(8,128)}, f32[1024,1024]{1,0:T(8,128)}, f32[1024,1024]{1,0:T(8,...) custom-call(bf16[1024,1024]{1,0:T(8,128)(2,1)S(1)} %get-tuple-element.13.emb, ...), custom_call_target="tpu_custom_call" | custom-call | tf_op jit(solution)/shard_map/widen/pallas_call | solution.py:916
Async XLA Ops:
  130.0 0.7 copy-start

commit v6 on v5

--- a/solution.py
+++ b/solution.py
@@ -267,7 +267,7 @@
     def __init__(self, hop, core, groups, held, inbox, total, sems):
         self.hop, self.core, self.groups = hop, core, groups
         self.held, self.inbox, self.total = held, inbox, total
-        self.send, self.recv, self.out, self.into, self.own = sems
+        self.send, self.recv, self.out, self.into = sems
         self.levels = len(groups[0][2])
         low, high = own_bit(hop, core, 2), own_bit(hop, core, 3)
         self.is_inner = low != high
@@ -324,10 +324,9 @@
 
     def up(self, group, level):
         kind, _, kept, size, _, _ = self.plans[group][level]
-        source = self.held if level == self.levels - 1 else self.total
         part = self.rows(kept, size)
         return pltpu.make_async_remote_copy(
-            src_ref=source.at[part],
+            src_ref=self.total.at[part],
             dst_ref=self.total.at[part],
             send_sem=self.out.at[group, level],
             recv_sem=self.into.at[group, level],
@@ -335,11 +334,6 @@
             device_id_type=MESH,
         )
 
-    def own_copy(self, group):
-        _, _, kept, size, _, _ = self.plans[group][-1]
-        part = self.rows(kept, size)
-        return pltpu.make_async_copy(self.held.at[part], self.total.at[part], self.own.at[group])
-
     def halve(self, group, level):
         self.when(self.roles(group, level, False)[0], lambda: self.down(group, level).start())
 
@@ -352,9 +346,9 @@
         def add():
             self.down(group, level).wait_recv()
             part = self.rows(kept, size)
-            self.held[part] = self.held[part] + self.inbox[pl.ds(place, size)]
+            done = self.total if level == self.levels - 1 else self.held
+            done[part] = self.held[part] + self.inbox[pl.ds(place, size)]
             if level == self.levels - 1:
-                self.own_copy(group).start()
                 self.up(group, level).start()
 
         self.when(self.roles(group, level, False)[1], add)
@@ -362,12 +356,7 @@
             self.halve(group, level + 1)
 
     def gather(self, group, level):
-        def take():
-            if level == self.levels - 1:
-                self.own_copy(group).wait()
-            self.up(group, level).wait_recv()
-
-        self.when(self.roles(group, level, True)[1], take)
+        self.when(self.roles(group, level, True)[1], lambda: self.up(group, level).wait_recv())
         if level > 0:
             self.double(group, level - 1)
 
@@ -383,16 +372,16 @@
 def layer_kernel(
     groups,
     child_in,
-    importance,
-    board,
-    slot,
-    counts,
+    importance_in,
+    board_in,
+    slot_in,
+    counts_in,
     parent_in,
     proj_in,
     q_in,
-    q_bias,
+    q_bias_in,
     w_in,
-    w_bias,
+    w_bias_in,
     cot_in,
     emb,
     message,
@@ -426,7 +415,14 @@
     info_in,
     bias_held,
     bias_in,
+    importance,
+    board,
+    slot,
+    counts,
+    q_bias,
+    w_bias,
     load_sem,
+    small_sem,
     info_sem,
     msg_sem,
     back_sem,
@@ -435,7 +431,6 @@
     sum_recv,
     sum_out,
     sum_in,
-    sum_own,
 ):
     hop, core = lax.axis_index("hop"), lax.axis_index("par")
     me = hop * 2 + core
@@ -472,7 +467,19 @@
         ((child_in, child), (proj_in, proj), (q_in, q), (parent_in, parent), (w_in, w), (cot_in, cot))
     ):
         loads.append(pltpu.make_async_copy(source, place, load_sem.at[index]))
-    for copy in loads[:3]:
+    small = []
+    for index, (source, place) in enumerate(
+        (
+            (importance_in, importance),
+            (board_in, board),
+            (slot_in, slot),
+            (counts_in, counts),
+            (q_bias_in, q_bias),
+            (w_bias_in, w_bias),
+        )
+    ):
+        small.append(pltpu.make_async_copy(source, place, small_sem.at[index]))
+    for copy in small + loads[:3]:
         copy.start()
 
     barrier = pltpu.get_barrier_semaphore()
@@ -487,6 +494,8 @@
     def column(row):
         return jnp.sum(jnp.where(eye, jnp.broadcast_to(row, (128, 128)), 0.0), axis=1, keepdims=True)
 
+    for copy in small:
+        copy.wait()
     count_row = counts[...].astype(f32)
     for part in range(slots // 128):
         owner = lax.broadcasted_iota(jnp.int32, (128, devices), 0) // cap + part * (128 // cap)
@@ -506,10 +515,13 @@
                 info[owner_at * cap : (owner_at + 1) * cap, :], axis=0, keepdims=True
             )
 
-    def send_info():
-        pl.semaphore_wait(barrier, devices - 1)
-
-        for to_hop, to_core in targets(0, devices // 2):
+    quarter = devices // 4
+
+    def targets_of(side_index):
+        return targets(quarter, 2 * quarter) if side_index == 0 else targets(0, quarter)
+
+    def send_info(side_index):
+        for to_hop, to_core in targets_of(side_index):
             pltpu.make_async_remote_copy(
                 src_ref=info_out.at[to_hop * 2 + to_core],
                 dst_ref=info_in.at[me],
@@ -518,11 +530,11 @@
                 device_id=(to_hop, to_core),
                 device_id_type=MESH,
             ).start()
-        pltpu.make_async_copy(info_out.at[me], info_in.at[me], info_sem.at[1]).start()
+        if side_index == 1:
+            pltpu.make_async_copy(info_out.at[me], info_in.at[me], info_sem.at[1]).start()
 
     def send_side(source, place_ref, sem, side_index):
-        quarter = devices // 4
-        for to_hop, to_core in targets(quarter, 2 * quarter) if side_index == 0 else targets(0, quarter):
+        for to_hop, to_core in targets_of(side_index):
             pltpu.make_async_remote_copy(
                 src_ref=source.at[rows_of(to_hop * 2 + to_core)],
                 dst_ref=place_ref.at[rows_of(me)],
@@ -572,7 +584,8 @@
             scaled_slope[rows, columns(tile)] = weights * (gate + act * (1.0 - gate))
 
         if side_index == 0:
-            send_info()
+            pl.semaphore_wait(barrier, devices - 1)
+        send_info(side_index)
         send_side(message, arrived, msg_sem, side_index)
 
     loads[3].wait()
@@ -668,7 +681,7 @@
 
         send_side(back_out, back_in, back_sem, side_index)
 
-    sums = Sums(hop, core, groups, held, inbox, total, (sum_send, sum_recv, sum_out, sum_in, sum_own))
+    sums = Sums(hop, core, groups, held, inbox, total, (sum_send, sum_recv, sum_out, sum_in))
     w_groups = [g for g, (first, _, _) in enumerate(groups) if first < 2 * width]
     q_groups = [g for g, (first, _, _) in enumerate(groups) if 2 * width <= first < 3 * width]
     p_groups = [g for g, (first, _, _) in enumerate(groups) if first >= 3 * width]
@@ -816,10 +829,10 @@
 
 GROUPS = [("cxyim", 2), ("cyxim", 2), ("cxyim", 2), ("cyxim", 2), ("cxyim", 4), ("cyxim", 4), ("cxyim", 4), ("cyxim", 4), ("cxyim", 4), ("cyxim", 4), ("cxyim", 4), ("cyxim", 4)]
 SCHEDULE = [
-    3, 4, 0, 1, 2, 0, 0, 3, 4, 0, 0, 0, 1, 2, 3, 4, 0, 5, 6, 0, 11, 12, 9, 10, 3, 4, 0, 1, 2, 7, 8, 3, 4, 5, 6, 1,
-    2, 11, 12, 3, 4, 9, 10, 5, 6, 1, 2, 7, 8, 11, 12, 3, 4, 9, 10, 7, 8, 5, 6, 1, 2, 3, 4, 11, 12, 1, 2, 9, 10, 5, 6, 7,
-    8, 5, 6, 11, 12, 1, 2, 5, 6, 9, 10, 11, 12, 7, 8, 9, 10, 11, 12, 3, 4, 9, 10, 7, 8, 7, 8, 5, 6, 11, 12, 1, 2, 9, 10, 5,
-    6, 7, 8, 3, 4, 11, 12, 9, 10, 7, 8, 5, 6, 1, 2, 11, 12, 9, 10, 7, 8,
+    1, 2, 0, 3, 4, 1, 0, 2, 0, 0, 0, 0, 4, 3, 1, 2, 0, 5, 0, 7, 8, 1, 2, 6, 4, 0, 7, 1, 5, 8, 2, 6, 11, 4, 12, 3,
+    10, 7, 2, 6, 9, 1, 3, 11, 5, 12, 4, 10, 3, 9, 2, 8, 7, 1, 6, 11, 5, 12, 3, 8, 9, 4, 11, 10, 1, 2, 8, 3, 7, 4, 9, 6,
+    5, 7, 12, 10, 5, 2, 6, 1, 9, 12, 4, 3, 11, 10, 5, 6, 9, 1, 8, 8, 12, 11, 7, 5, 12, 6, 9, 10, 7, 11, 3, 2, 5, 12, 10, 4,
+    9, 8, 12, 11, 6, 10, 9, 7, 3, 8, 4, 6, 9, 12, 11, 10, 5, 8, 10, 11, 7,
 ]
 
 
@@ -854,14 +867,21 @@
     q_bias_out,
     w_out,
     w_bias_out,
-    narrow,
     wide,
-    read_sem,
+    w_bias,
+    q_bias,
     write_sem,
-    child_sem,
+    other_sem,
 ):
-    slots, rows, width = narrow.shape
-    through = pltpu.make_async_copy(child, child_out, child_sem)
+    slots, rows, width = wide.shape
+    w_bias[...] = biases[0, :]
+    q_bias[...] = biases[1, :]
+    others = [
+        pltpu.make_async_copy(source, place, other_sem.at[index])
+        for index, (source, place) in enumerate(((child, child_out), (w_bias, w_bias_out), (q_bias, q_bias_out)))
+    ]
+    for copy in others:
+        copy.start()
     pieces = []
     for source, place in ((parent, parent_out), (emb, emb_out)):
         for first in range(0, place.shape[0], rows):
@@ -871,45 +891,25 @@
         for first in range(0, place.shape[0], rows):
             pieces.append((total, base + first, place, first))
         base += place.shape[0]
-    near = [True for source, _, _, _ in pieces]
-
-    def read(index):
-        source, first, _, _ = pieces[index]
-        slot = index % slots
-        return pltpu.make_async_copy(source.at[pl.ds(first, rows)], narrow.at[slot], read_sem.at[slot])
-
     def write(index):
         _, _, place, first = pieces[index]
         slot = index % slots
         return pltpu.make_async_copy(wide.at[slot], place.at[pl.ds(first, rows)], write_sem.at[slot])
 
-    far = [index for index in range(len(pieces)) if not near[index]]
-    for index in far[:slots]:
-        read(index).start()
-    for index in range(len(pieces)):
-        source, first, _, _ = pieces[index]
+    for index, (source, first, _, _) in enumerate(pieces):
         if index >= slots:
             write(index - slots).wait()
-        if near[index]:
-            value = source[first : first + rows, :]
-        else:
-            read(index).wait()
-            value = narrow[index % slots]
-        wide[index % slots] = value.astype(jnp.float32)
+        wide[index % slots] = source[first : first + rows, :].astype(jnp.float32)
         write(index).start()
-        if not near[index] and index + slots < len(pieces):
-            read(index + slots).start()
-    through.start()
-    w_bias_out[...] = biases[0, :]
-    q_bias_out[...] = biases[1, :]
     for index in range(len(pieces) - slots, len(pieces)):
         write(index).wait()
-    through.wait()
+    for copy in others:
+        copy.wait()
 
 
 def widen(emb, child, parent, total, biases):
     width = emb.shape[1]
-    slots, rows = 4, 512
+    slots, rows = 8, 256
     shape, f32 = jax.ShapeDtypeStruct, jnp.float32
     hbm = pl.BlockSpec(memory_space=pl.ANY)
     vmem = pl.BlockSpec(memory_space=pltpu.VMEM)
@@ -927,13 +927,13 @@
             shape((width,), f32),
         ),
         in_specs=[vmem, vmem, vmem, vmem, vmem],
-        out_specs=(hbm, hbm, hbm, hbm, hbm, vmem, hbm, vmem),
+        out_specs=(hbm,) * 8,
         scratch_shapes=[
-            pltpu.VMEM((slots, rows, width), child.dtype),
             pltpu.VMEM((slots, rows, width), f32),
+            pltpu.VMEM((width,), f32),
+            pltpu.VMEM((width,), f32),
             pltpu.SemaphoreType.DMA((slots,)),
-            pltpu.SemaphoreType.DMA((slots,)),
-            pltpu.SemaphoreType.DMA,
+            pltpu.SemaphoreType.DMA((3,)),
         ],
         compiler_params=pltpu.CompilerParams(vmem_limit_bytes=36 << 20),
     )(emb, child, parent, total, biases)
@@ -971,9 +971,9 @@
             pltpu.VMEM((slots, width), bf16),
             pltpu.VMEM((parents, width), bf16),
             pltpu.VMEM((4 * width, width), bf16),
-            shape((2, width), f32),
+            pltpu.VMEM((2, width), f32),
         ),
-        in_specs=[hbm, vmem, vmem, vmem, vmem, hbm, hbm, hbm, vmem, hbm, vmem, hbm],
+        in_specs=[hbm] * 12,
         out_specs=(vmem, vmem, vmem, vmem, vmem),
         scratch_shapes=[
             pltpu.VMEM((slots, width), bf16),
@@ -1003,14 +1003,20 @@
             pltpu.VMEM((devices, 1, 128), f32),
             pltpu.VMEM((levels, 2, width), f32),
             pltpu.VMEM((levels, 2, width), f32),
+            pltpu.VMEM((slots // 128, 128), f32),
+            pltpu.VMEM((slots // 128, 128), jnp.int32),
+            pltpu.VMEM((slots // 128, 128), jnp.int32),
+            pltpu.VMEM(send_counts.shape, jnp.int32),
+            pltpu.VMEM((1, width), f32),
+            pltpu.VMEM((1, width), f32),
+            dma((6,)),
             dma((6,)),
             dma((2,)),
             dma((2, 2)),
             dma((2, 2)),
             dma((2, levels)),
         ]
-        + [dma((len(groups), len(groups[0][2])))] * 4
-        + [dma((len(groups),))],
+        + [dma((len(groups), len(groups[0][2])))] * 4,
         compiler_params=pltpu.CompilerParams(
             collective_id=1, has_side_effects=True, vmem_limit_bytes=50 << 20
         ),

time: 141 us -> 137 us (0.972)
  Pallas kernels: 139 us -> 136 us
    pallas_call x1, Pallas kernels: 129 us -> 127 us  [fused_body(): pl.pallas_call(functools.partial(layer_kernel, groups), name='layer', out...]
where the time goes in v6:
time: 137 us
  Pallas kernels  136 us (99%)
    pallas_call x1, Pallas kernels, fused_body(): pl.pallas_call(functools.partial(layer_kernel, groups), name='layer', out...  127 us
    pallas_call x1, Pallas kernels, widen(): pl.pallas_call(widen_kernel, name='widen', out_shape=(shape(emb.shape, f3...  8.77 us

profile of v6, /device:TPU:0, one launch (start us, length us, event | category | flops | bytes accessed | tf_op | source)
XLA Modules:
  0.0 136.8 jit_solution(8724092019225985946)
XLA Ops:
  0.6 127.2 %layer.1 = (bf16[1024,1024]{1,0:T(8,128)(2,1)S(1)}, bf16[512,1024]{1,0:T(8,128)(2,1)S(1)}, bf16[1024,1024]{1,0:T(8,128)(2,1)S(1)}, bf16[4096,1024]{1,0:T(8,128)(2,1)S(1)}, f32[2,1024]{1,0:T(2,128)S(1)}) custom-call(bf16[512,1024]{1,0:T(8,128)(2,1)} %child_in.1, f32[4,128]{1,0:T(4,128)} %bitcast.7, s32[4,128]{1,0:T(4,128)} %bitcast.8, s32[4,128]{1,0:T(4,128)} %bitcast.9, ...), custom_call_target="tpu_custom_call" | custom-call | flops 19327352832 | bytes 41943040 | tf_op jit(solution)/shard_map/layer/pallas_call | solution.py:966
  127.9 8.8 %widen.1 = (f32[1024,1024]{1,0:T(8,128)}, bf16[512,1024]{1,0:T(8,128)(2,1)}, f32[1024,1024]{1,0:T(8,128)}, f32[1024,1024]{1,0:T(8,128)}, f32[1024,1024]{1,0:T(8,...) custom-call(bf16[1024,1024]{1,0:T(8,128)(2,1)S(1)} %get-tuple-element.13.emb, ...), custom_call_target="tpu_custom_call" | custom-call | tf_op jit(solution)/shard_map/widen/pallas_call | solution.py:916

commit v7 on v6

--- a/solution.py
+++ b/solution.py
@@ -244,6 +244,7 @@
 
 
 TILE = 512
+WIDE = 1024
 BLOCK = 128
 
 
@@ -441,6 +442,7 @@
     half = slots // 2
     levels = bias_held.shape[0]
     tiles = width // TILE
+    wides = width // WIDE
     upper = own_bit(hop, core, levels - 2)
     sides = (1 - upper, upper)
     f32, bf16 = jnp.float32, jnp.bfloat16
@@ -666,18 +668,18 @@
 
     for side_index, side in enumerate(sides):
         rows = side_rows(side)
-        shrinks = spread(slot_shrink[rows, :], TILE)
-
-        @pl.loop(0, tiles)
+        shrinks = spread(slot_shrink[rows, :], WIDE)
+
+        @pl.loop(0, wides)
         def _(tile):
-            grad_moved[rows, columns(tile)] = (
-                shrinks * mm(table_rows[rows, :], grad_pre[:, columns(tile)])
+            grad_moved[rows, columns(tile, WIDE)] = (
+                shrinks * mm(table_rows[rows, :], grad_pre[:, columns(tile, WIDE)])
             ).astype(bf16)
 
-        @pl.loop(0, tiles)
+        @pl.loop(0, wides)
         def _(tile):
-            turned = w[pl.ds(pl.multiple_of(width + tile * TILE, TILE), TILE), :]
-            back_out[rows, columns(tile)] = times_transpose(grad_moved[rows, :], turned).astype(bf16)
+            turned = w[pl.ds(pl.multiple_of(width + tile * WIDE, WIDE), WIDE), :]
+            back_out[rows, columns(tile, WIDE)] = times_transpose(grad_moved[rows, :], turned).astype(bf16)
 
         send_side(back_out, back_in, back_sem, side_index)
 

time: 137 us -> 136 us (level)
  no operation moved by 1% of the time
where the time goes in v7:
time: 136 us
  Pallas kernels  135 us (99%)
    pallas_call x1, Pallas kernels, fused_body(): pl.pallas_call(functools.partial(layer_kernel, groups), name='layer', out...  126 us
    pallas_call x1, Pallas kernels, widen(): pl.pallas_call(widen_kernel, name='widen', out_shape=(shape(emb.shape, f3...  8.77 us

profile of v7, /device:TPU:0, one launch (start us, length us, event | category | flops | bytes accessed | tf_op | source)
XLA Modules:
  0.0 135.6 jit_solution(13944316323570110229)
XLA Ops:
  0.6 126.1 %layer.1 = (bf16[1024,1024]{1,0:T(8,128)(2,1)S(1)}, bf16[512,1024]{1,0:T(8,128)(2,1)S(1)}, bf16[1024,1024]{1,0:T(8,128)(2,1)S(1)}, bf16[4096,1024]{1,0:T(8,128)(2,1)S(1)}, f32[2,1024]{1,0:T(2,128)S(1)}) custom-call(bf16[512,1024]{1,0:T(8,128)(2,1)} %child_in.1, f32[4,128]{1,0:T(4,128)} %bitcast.7, s32[4,128]{1,0:T(4,128)} %bitcast.8, s32[4,128]{1,0:T(4,128)} %bitcast.9, ...), custom_call_target="tpu_custom_call" | custom-call | flops 19327352832 | bytes 41943040 | tf_op jit(solution)/shard_map/layer/pallas_call | solution.py:968
  126.7 8.8 %widen.1 = (f32[1024,1024]{1,0:T(8,128)}, bf16[512,1024]{1,0:T(8,128)(2,1)}, f32[1024,1024]{1,0:T(8,128)}, f32[1024,1024]{1,0:T(8,128)}, f32[1024,1024]{1,0:T(8,...) custom-call(bf16[1024,1024]{1,0:T(8,128)(2,1)S(1)} %get-tuple-element.13.emb, ...), custom_call_target="tpu_custom_call" | custom-call | tf_op jit(solution)/shard_map/widen/pallas_call | solution.py:918
